TPU v7x, 512 devices: a whole 4x8x8 slice. The times are simulated.
512 devices in a mesh: region: 32 (over x, z), mp: 16 (over y, core).
Axes of the slice: x: 4, y: 8, z: 8, core: 2. Of those that a mesh axis runs over, the one named last changes fastest.
Arguments:
- tokens: bfloat16 [32768, 1024], P('region', 'mp'), may hold values from -6 to 6
- cotangent: bfloat16 [32768, 1024], P('region', 'mp'), may hold values from -6 to 6
- gain: float32 [1024], replicated, may hold values from 0.1 to 1.9
- w_up: bfloat16 [1024, 4096], P(None, 'mp'), may hold values from -0.1875 to 0.1875
- w_down: bfloat16 [4096, 1024], P('mp'), may hold values from -0.09375 to 0.09375
- counts: int32 [128], P('region'), may hold values from 16 to 256, as said below
Outputs:
- d_tokens: bfloat16 [32768, 1024], P('region', 'mp')
- d_up: float32 [1024, 4096], P('region', 'mp')
- d_down: float32 [4096, 1024], P('mp', 'region')
- d_gain: float32 [1024], P('mp')
Inputs may be any that keep to these rules, and one draw needn't show every extreme that they name: `counts`: each count is 16 times 1 + 3k for a whole k. Every group of 16 consecutive regions holds 1984 tokens, so all regions hold 15872 tokens together. The 4 regions of one owner hold at most 1024 tokens, and some owner holds exactly 1024 in every draw.
All inputs are finite; a program needn't handle non-finite values.
Results may differ from a plain program's by a relative error of at most 0.015.
Values may be sent and summed in bfloat16 or wider, within the bound.
A program may use at most 64 MiB of HBM per device.

v0:
```python
import math

import jax
import jax.numpy as jnp
from jax import lax
from jax.sharding import Mesh
from jax.sharding import PartitionSpec as P

BAL = 496
MP = ("mp_0", "mp_1")


EPSILON = 1e-05


def turned_gather(arrays, axis, dims):
    turned = [jnp.moveaxis(a, dim, 0) for a, dim in zip(arrays, dims)]
    widths = [t[0].size for t in turned]
    both = jnp.concatenate([t.reshape(-1, w) for t, w in zip(turned, widths)], axis=1)
    whole = lax.all_gather(both, axis, axis=0, tiled=True)
    blocks = jnp.split(whole, [sum(widths[:k]) for k in range(1, len(widths))], axis=1)
    return tuple(
        (
            jnp.moveaxis(b.reshape(-1, *t.shape[1:]), 0, dim)
            for b, t, dim in zip(blocks, turned, dims)
        )
    )


def split_up(value, dim, length):
    lengths = value.shape
    blocks = value.reshape(*lengths[:dim], length, lengths[dim] // length, *lengths[dim + 1 :])
    return jnp.moveaxis(blocks, dim, 0)


def sum_by_chip(value, chips, core, dim):
    sizes = (lax.axis_size(chips), lax.axis_size(core))
    blocks = split_up(value, dim, sizes[0] * sizes[1])
    inside = blocks.shape[1:]
    blocks = blocks.reshape(*sizes, *inside).swapaxes(0, 1).reshape(-1, *inside)
    blocks = lax.psum_scatter(blocks, core, scatter_dimension=0, tiled=True)
    return lax.psum_scatter(blocks, chips, scatter_dimension=0, tiled=True)[0]


def from_everyone(value, axis):
    length = lax.axis_size(axis)
    return lax.all_to_all(
        jnp.broadcast_to(value[None], (length, *value.shape)), axis, 0, 0, tiled=True
    )


def taken_together(value, axis):
    return from_everyone(value, axis).sum(axis=0)


def sum_at_owner(value, axis, dim):
    length = lax.axis_size(axis)
    blocks = lax.all_to_all(split_up(value, dim, length), axis, 0, 0, tiled=True)
    return jnp.sum(blocks.astype(jnp.float32), axis=0)


def gelu_tanh(inputs):
    return jax.nn.gelu(inputs, approximate=True)


def backward(rows_x, rows_dy, live_rows, gain, w_up, w_down, grad_scale):
    whole_x, whole_dy = turned_gather((rows_x, rows_dy), MP, (1, 1))
    share_width = rows_x.shape[1]
    feature_count = whole_x.shape[1]
    whole_float = whole_x.astype(jnp.float32)
    inv_rms = lax.rsqrt(jnp.mean(whole_float * whole_float, axis=1) + EPSILON)
    normed = (whole_float * inv_rms[:, None] * gain).astype(jnp.bfloat16)
    hidden = jnp.dot(normed, w_up, preferred_element_type=jnp.float32)
    activated, gelu_back = jax.vjp(gelu_tanh, hidden)
    act_rows = (activated * live_rows[:, None]).astype(jnp.bfloat16)
    d_act = lax.dot_general(
        whole_dy, w_down, (((1,), (1,)), ((), ())), preferred_element_type=jnp.float32
    )
    d_hidden = (gelu_back(d_act)[0] * live_rows[:, None]).astype(jnp.bfloat16)
    partial_term = lax.dot_general(
        d_hidden, w_up, (((1,), (1,)), ((), ())), preferred_element_type=jnp.float32
    )
    d_normed = sum_by_chip(partial_term.astype(jnp.bfloat16), "mp_0", "mp_1", 1).astype(jnp.float32)
    offset = lax.axis_index(MP) * share_width
    gain_part = lax.dynamic_slice_in_dim(gain, offset, share_width)
    x_part = rows_x.astype(jnp.float32)
    weighted = gain_part * d_normed
    row_dot = taken_together(jnp.sum(weighted * x_part, axis=1), MP)
    cubed = inv_rms * inv_rms * inv_rms
    d_rows = (
        rows_dy.astype(jnp.float32)
        + weighted * inv_rms[:, None]
        - x_part * (row_dot * cubed / feature_count)[:, None]
    )
    d_rows = (d_rows * live_rows[:, None]).astype(jnp.bfloat16)
    gain_term = jnp.sum(d_normed * x_part * (inv_rms * live_rows)[:, None], axis=0) * grad_scale
    up_term = lax.dot_general(
        normed, d_hidden, (((0,), (0,)), ((), ())), preferred_element_type=jnp.float32
    )
    down_term = lax.dot_general(
        whole_dy, act_rows, (((0,), (0,)), ((), ())), preferred_element_type=jnp.float32
    )
    grads = jnp.stack([up_term, down_term]) * grad_scale
    grads_part = sum_at_owner(grads.astype(jnp.bfloat16), "region", 1)
    gain_grad = taken_together(gain_term, "region")
    return (d_rows, grads_part, gain_grad)


def on_device(tokens, cotangent, gain, w_up, w_down, counts):
    regions_n = lax.axis_size("region")
    rows_cap = tokens.shape[0]
    grad_scale = 1.0 / math.sqrt(BAL * regions_n)
    own_load = jnp.sum(counts)
    own_rows = jnp.arange(rows_cap, dtype=jnp.int32)
    live_rows = (own_rows < own_load).astype(jnp.float32)
    d_tokens, grads_part, gain_grad = backward(
        tokens, cotangent, live_rows, gain, w_up, w_down, grad_scale
    )
    return (d_tokens, grads_part[0], grads_part[1].T, gain_grad)


def solution(mesh):
    torus = Mesh(mesh.devices.reshape(mesh.shape["region"], 8, 2), ("region", "mp_0", "mp_1"))
    in_specs = (P("region", MP), P("region", MP), P(), P(None, MP), P(MP, None), P("region"))
    out_specs = (P("region", MP), P("region", MP), P(MP, "region"), P(MP))
    return jax.shard_map(
        on_device, mesh=torus, in_specs=in_specs, out_specs=out_specs, check_vma=False
    )
```

profile of v0, /device:TPU:1, one launch (start us, length us, event | category | flops | bytes accessed | tf_op | source)
XLA Modules:
  0.0 175.7 jit_solution(16805085722291044228)
XLA Ops:
  7.2 0.0 copy-start
  7.2 0.0 all-gather.2.cloned.1.call-start
  7.2 1.7 pad_maximum_fusion
  8.9 0.0 all-gather.2.cloned.1.call-update
  9.0 0.0 reduce-scatter.3.cloned.1.call-start
  9.0 1.3 reduce_sum.64
  10.3 0.6 fusion.39
  11.0 49.7 %all-gather.2.cloned.1.call-done = bf16[1024,2048]{1,0:T(8,128)(2,1)} async-done(((bf16[64,2048]{1,0:T(8,128)(2,1)}), bf16[1024,2048]{1,0:T(8,128)(2,1)}) %all-gather.2.cloned.1.call-update) | async-done | bytes 4194320 | tf_op jit(solution)/shard_map/all_gather | solution.py:20
  60.6 2.1 %fusion = f32[1024]{0:T(1024)S(1)} fusion(bf16[1024,2048]{1,0:T(8,128)(2,1)} %all-gather.2.cloned.1.call-done), kind=kLoop, calls=%fused_computation.2 | loop fusion | flops 3144704 | bytes 2101248 | tf_op jit(solution)/shard_map/reduce_sum | solution.py:71
  62.7 0.6 fusion.38
  63.4 0.0 copy-done
  63.4 0.0 copy-start.2
  63.4 0.0 copy-start.4
  63.4 2.7 %fusion.26 = f32[1024,256]{1,0:T(8,128)S(1)} fusion(bf16[1024,256]{1,0:T(8,128)(2,1)S(1)} %copy-done, f32[1024]{0:T(1024)} %param.8, f32[1024]{0:T(1024)S(1)} %get-tuple-element.9, bf16[1024,2048]{1,0:T(8,128)(2,1)} %all-gather.2.cloned.1.call-done), kind=kOutput, calls=%fused_computation.34 | convolution fusion | flops 541065216 | bytes 3678208 | tf_op jit(solution)/shard_map/dot_general | solution.py:73
  66.1 0.1 copy-done.2
  66.2 0.1 copy-done.4
  66.3 1.3 fusion.15
  67.7 0.7 convolution_convert_fusion
  68.4 1.5 copy.17
  69.9 0.0 reduce-scatter.3.cloned.1.call-update
  69.9 0.0 copy-start.5
  70.0 0.0 reduce-scatter.5.cloned.1.call-start
  70.0 2.5 %fusion.4 = f32[1024,256]{1,0:T(8,128)S(1)} fusion(bf16[1024,2048]{1,0:T(8,128)(2,1)} %all-gather.2.cloned.1.call-done, f32[1024,256]{1,0:T(8,128)S(1)} %fusion.26, f32[1024]{0:T(1024)S(1)} %fusion.39), kind=kOutput, calls=%fused_computation.9 | convolution fusion | flops 539492352 | bytes 4198400 | tf_op jit(solution)/shard_map/dot_general | solution.py:100
  72.5 15.5 %reduce-scatter.3.cloned.1.call-done = bf16[8,1024,64]{1,2,0:T(8,128)(2,1)} async-done(((bf16[16,1024,64]{1,2,0:T(8,128)(2,1)}), bf16[8,1024,64]{1,2,0:T(8,128)(2,1)}) %reduce-scatter.3.cloned.1.call-update) | async-done | bytes 1048592 | tf_op jit(solution)/shard_map/reduce_scatter | solution.py:41
  87.9 0.0 reduce-scatter.5.cloned.1.call-update
  87.9 0.0 copy-done.5
  88.0 2.4 %fusion.24 = f32[1024,256]{1,0:T(8,128)S(1)} fusion(bf16[1024,256]{1,0:T(8,128)(2,1)S(1)} %fusion.15, f32[1024]{0:T(1024)S(1)} %copy-done.5, f32[1024]{0:T(1024)S(1)} %get-tuple-element.9, bf16[1024,2048]{1,0:T(8,128)(2,1)} %all-gather.2.cloned.1.call-done), kind=kOutput, calls=%fused_computation.33 | convolution fusion | flops 541065216 | bytes 3678208 | tf_op jit(solution)/shard_map/dot_general | solution.py:97
  90.3 0.0 copy-start.1
  90.3 0.0 copy-start.3
  90.3 1.3 fusion.16
  91.6 9.0 %all-to-all-start.1 = ((bf16[32,2,32,256]{3,2,1,0:T(8,128)(2,1)}), bf16[32,2,32,256]{3,2,1,0:T(8,128)(2,1)S(1)}, u32[]{:S(2)}, u32[]{:S(2)}) async-start(bf16[32,2,32,256]{3,2,1,0:T(8,128)(2,1)} %fusion.16), calls=%async_computation.3 | async-start | bytes 2097152 | tf_op jit(solution)/shard_map/all_to_all | solution.py:58
  100.7 0.1 dynamic_slice.3
  100.7 27.4 %reduce-scatter.5.cloned.1.call-done = bf16[1,1024,64]{1,2,0:T(8,128)(2,1)} async-done(((bf16[8,1024,64]{1,2,0:T(8,128)(2,1)}), bf16[1,1024,64]{1,2,0:T(8,128)(2,1)}) %reduce-scatter.5.cloned.1.call-update) | async-done | bytes 131088 | tf_op jit(solution)/shard_map/reduce_scatter | solution.py:42
  128.1 0.0 copy-done.1
  128.1 1.1 fusion.35
  129.2 0.0 all-to-all-done.1
  129.3 0.6 broadcast_in_dim.5
  129.9 9.8 %all-to-all-start.2 = ((f32[32,1,64]{2,1,0:T(1,128)}), f32[32,1,64]{2,1,0:T(1,128)S(1)}, u32[]{:S(2)}, u32[]{:S(2)}) async-start(f32[32,1,64]{2,1,0:T(1,128)} %broadcast_in_dim.5), calls=%async_computation.4 | async-start | bytes 32768 | tf_op jit(solution)/shard_map/all_to_all | solution.py:47
  139.7 0.2 convert_reduce_fusion
  139.8 8.4 %all-to-all-done.2 = f32[32,1,64]{2,1,0:T(1,128)S(1)} async-done(((f32[32,1,64]{2,1,0:T(1,128)}), f32[32,1,64]{2,1,0:T(1,128)S(1)}, u32[]{:S(2)}, u32[]{:S(2)}) %all-to-all-start.2) | async-done | bytes 8224 | tf_op jit(solution)/shard_map/all_to_all | solution.py:47
  148.2 0.7 broadcast_in_dim.4
  148.9 10.6 %all-to-all-start = ((f32[16,1,1024]{2,1,0:T(1,128)}), f32[16,1,1024]{2,1,0:T(1,128)S(1)}, u32[]{:S(2)}, u32[]{:S(2)}) async-start(f32[16,1,1024]{2,1,0:T(1,128)} %broadcast_in_dim.4), calls=%async_computation.2 | async-start | bytes 131072 | tf_op jit(solution)/shard_map/all_to_all | solution.py:47
  159.6 0.6 slice_bitcast_fusion
  160.2 0.5 reduce_sum.69
  160.7 6.6 %all-to-all-done = f32[16,1,1024]{2,1,0:T(1,128)S(1)} async-done(((f32[16,1,1024]{2,1,0:T(1,128)}), f32[16,1,1024]{2,1,0:T(1,128)S(1)}, u32[]{:S(2)}, u32[]{:S(2)}) %all-to-all-start) | async-done | bytes 65568 | tf_op jit(solution)/shard_map/all_to_all | solution.py:47
  167.4 0.1 reduce_sum.66
  167.4 0.0 copy-done.3
  167.4 1.7 fusion.32
  (2 shorter events, 0.0 us)
Async XLA Ops:
  7.2 56.2 %copy-start = (bf16[1024,256]{1,0:T(8,128)(2,1)S(1)}, bf16[1024,256]{1,0:T(8,128)(2,1)}, u32[]{:S(2)}) copy-start(bf16[1024,256]{1,0:T(8,128)(2,1)} %param.9) | copy-start | bytes 1572868
  7.2 53.5 %all-gather.2.cloned.1.call-start = ((), (), s32[]{:S(2)}) async-start(), calls=%async_computation.5 | async-start | bytes 4456448 | tf_op jit(solution)/shard_map/all_gather | solution.py:20
  9.0 78.9 %reduce-scatter.3.cloned.1.call-start = ((), (), s32[]{:S(2)}) async-start(), calls=%async_computation.6 | async-start | bytes 3145728 | tf_op jit(solution)/shard_map/reduce_scatter | solution.py:41
  63.4 2.8 %copy-start.2 = (bf16[1024,2048]{1,0:T(8,128)(2,1)S(1)}, bf16[1024,2048]{1,0:T(8,128)(2,1)}, u32[]{:S(2)}) copy-start(bf16[1024,2048]{1,0:T(8,128)(2,1)} %all-gather.2.cloned.1.call-done) | copy-start | bytes 12582916
  63.4 2.9 %copy-start.4 = (bf16[256,1024]{1,0:T(8,128)(2,1)S(1)}, bf16[256,1024]{1,0:T(8,128)(2,1)}, u32[]{:S(2)}) copy-start(bf16[256,1024]{1,0:T(8,128)(2,1)} %param.10) | copy-start | bytes 1572868
  69.9 18.0 %copy-start.5 = (f32[1024]{0:T(1024)S(1)}, f32[1024]{0:T(1024)}, u32[]{:S(2)}) copy-start(f32[1024]{0:T(1024)} %param.8) | copy-start | bytes 12292
  70.0 58.1 %reduce-scatter.5.cloned.1.call-start = ((), (), s32[]{:S(2)}) async-start(), calls=%async_computation.7 | async-start | bytes 1179648 | tf_op jit(solution)/shard_map/reduce_scatter | solution.py:42
  90.3 37.8 %copy-start.1 = (bf16[1024,64]{0,1:T(8,128)(2,1)S(1)}, bf16[1024,64]{0,1:T(8,128)(2,1)}, u32[]{:S(2)}) copy-start(bf16[1024,64]{0,1:T(8,128)(2,1)} %param.6) | copy-start | bytes 393220
  90.3 77.1 %copy-start.3 = (bf16[1024,64]{0,1:T(8,128)(2,1)S(1)}, bf16[1024,64]{0,1:T(8,128)(2,1)}, u32[]{:S(2)}) copy-start(bf16[1024,64]{0,1:T(8,128)(2,1)} %param.7) | copy-start | bytes 393220
  91.6 37.6 %all-to-all-start.1 = ((bf16[32,2,32,256]{3,2,1,0:T(8,128)(2,1)}), bf16[32,2,32,256]{3,2,1,0:T(8,128)(2,1)S(1)}, u32[]{:S(2)}, u32[]{:S(2)}) async-start(bf16[32,2,32,256]{3,2,1,0:T(8,128)(2,1)} %fusion.16), calls=%async_computation.3 | async-start | bytes 2097152 | tf_op jit(solution)/shard_map/all_to_all | solution.py:58
  129.9 18.4 %all-to-all-start.2 = ((f32[32,1,64]{2,1,0:T(1,128)}), f32[32,1,64]{2,1,0:T(1,128)S(1)}, u32[]{:S(2)}, u32[]{:S(2)}) async-start(f32[32,1,64]{2,1,0:T(1,128)} %broadcast_in_dim.5), calls=%async_computation.4 | async-start | bytes 32768 | tf_op jit(solution)/shard_map/all_to_all | solution.py:47
  148.9 18.5 %all-to-all-start = ((f32[16,1,1024]{2,1,0:T(1,128)}), f32[16,1,1024]{2,1,0:T(1,128)S(1)}, u32[]{:S(2)}, u32[]{:S(2)}) async-start(f32[16,1,1024]{2,1,0:T(1,128)} %broadcast_in_dim.4), calls=%async_computation.2 | async-start | bytes 131072 | tf_op jit(solution)/shard_map/all_to_all | solution.py:47
Sparse Core Ops, SparseCore 0:
  10.1 50.4 all-gather.1
  70.1 17.8 reduce-scatter.2
  91.0 37.0 reduce-scatter.4
where the time goes:
time: 176 us
  waiting for transfers between devices  108 us (61%)
  starting transfers between devices  29.6 us (17%)
  between operations  13.9 us (8%)
  other arithmetic  11.2 us (6%)
  matrix products  9.63 us (5%)
  local copies, waits for them, and re-layouts  3.7 us (2%)
    all_gather x1, waiting for transfers between devices, turned_gather(): whole = lax.all_gather(both, axis, axis=0, tiled=True)  49.7 us
    reduce_scatter x1, waiting for transfers between devices, sum_by_chip(): return lax.psum_scatter(blocks, chips, scatter_dimension=0, tiled=True)[0]  27.4 us
    all_to_all x2, starting transfers between devices, from_everyone(): lax.all_to_all(jnp.broadcast_to(value[None], (length, *value.shape)), axi...  20.4 us
    reduce_scatter x1, waiting for transfers between devices, sum_by_chip(): blocks = lax.psum_scatter(blocks, core, scatter_dimension=0, tiled=True)  15.5 us
    all_to_all x2, waiting for transfers between devices, from_everyone(): lax.all_to_all(jnp.broadcast_to(value[None], (length, *value.shape)), axi...  15 us
    all_to_all x1, starting transfers between devices, sum_at_owner(): lax.all_to_all(split_up(value, dim, length), axis, 0, 0, tiled=True)  9.03 us
  transfers between devices with their start and end apart: 6, of which 5 were waited for; matrix products, arithmetic and copies ran while one was open for 6% of the time, Pallas kernels for 0%

commit v1 on v0

v1 whole, which is shorter than its diff:
```python
import functools
import math

import jax
import jax.numpy as jnp
from jax import lax
from jax.experimental import pallas as pl
from jax.experimental.pallas import tpu as pltpu
from jax.sharding import PartitionSpec as P

BAL = 496
EPSILON = 1e-05
MESH = pl.DeviceIdType.MESH
F32 = jnp.float32
BF16 = jnp.bfloat16
NCH = 4
GC = math.sqrt(2.0 / math.pi)


def nt_dot(a, b):
    return lax.dot_general(a, b, (((1,), (1,)), ((), ())), preferred_element_type=F32)


def nn_dot(a, b):
    return lax.dot_general(a, b, (((1,), (0,)), ((), ())), preferred_element_type=F32)


def kernel(
    X, Z, Y, s,
    x_hbm, d_hbm, gain_ref, wu_hbm, wd_hbm, counts_ref,
    dtok_ref, dup_ref, ddn_ref, dgain_ref,
    B, wu, wd, wg, wgT, gainb, Q, Qs, RSs, RSr, U, V, Gs, Xr, Ss, Zr,
    g1, g1r, g2, gy, g3, gx, g4, gz, live_s,
    loc, ag_s, ag_r, sb_s, sb_r, qs_s, qs_r, rs_s, rs_r, x_s, x_r, z_s, z_r,
    ga_s, ga_r, gy_s, gy_r, gx_s, gx_r, gz_s, gz_r,
):
    r = lax.axis_index("region")
    m = lax.axis_index("mp")
    x, z = r // Z, r % Z
    y, c = m // 2, m % 2
    H2 = Y // 2
    TC = B.shape[3]
    FB = B.shape[2] // 2
    D = wu.shape[0]
    FH = wu.shape[1]
    sib = (r, y * 2 + 1 - c)

    def ydev(k):
        return (r, ((y + k + Y) % Y) * 2 + c)

    def xdev(k):
        return (((x + k) % X) * Z + z, m)

    def zdev(k):
        return (x * Z + (z + k) % Z, m)

    bar = pltpu.get_barrier_semaphore()
    peers = [sib] + [ydev(k) for k in range(1, Y)] + [xdev(k) for k in range(1, X)]
    peers += [zdev(k) for k in range(1, Z)]
    for p in peers:
        pl.semaphore_signal(bar, 1, device_id=p, device_id_type=MESH)

    own = []
    for k in range(NCH):
        lanes = pl.ds(k * TC, TC)
        own.append(pltpu.make_async_copy(x_hbm.at[:, lanes], B.at[k, m, pl.ds(0, FB)], loc.at[2 * k]))
        own.append(pltpu.make_async_copy(d_hbm.at[:, lanes], B.at[k, m, pl.ds(FB, FB)], loc.at[2 * k + 1]))
    wcp = [
        pltpu.make_async_copy(wu_hbm, wu, loc.at[2 * NCH]),
        pltpu.make_async_copy(wd_hbm, wd, loc.at[2 * NCH + 1]),
    ]
    for cp in own + wcp:
        cp.start()
    load = counts_ref[0] + counts_ref[1] + counts_ref[2] + counts_ref[3]
    for k in range(NCH):
        at = lax.broadcasted_iota(jnp.int32, (1, TC), 1) + k * TC
        live_s[k] = jnp.where(at < load, 1.0, 0.0).astype(F32)
    for cp in own:
        cp.wait()
    pl.semaphore_wait(bar, len(peers))

    pending = []

    def remote(src, dst, ss, rs, dev):
        return pltpu.make_async_remote_copy(
            src_ref=src, dst_ref=dst, send_sem=ss, recv_sem=rs, device_id=dev, device_id_type=MESH
        )

    def go(cp):
        cp.start()
        pending.append(cp)

    def ag(d, h, k):
        sg = 1 if d == 0 else -1
        slot = ((y - sg * (h - 1) + Y) % Y) * 2 + c
        ref = B.at[k, slot] if h < H2 else B.at[k, slot, pl.ds(d * FB, FB)]
        return remote(ref, ref, ag_s.at[d, h - 1, k], ag_r.at[d, h - 1, k], ydev(sg))

    def sb(j, k):
        ref = B.at[k, ((y + j + Y) % Y) * 2 + c]
        return remote(ref, ref, sb_s.at[j % Y, k], sb_r.at[j % Y, k], sib)

    def own_send(k):
        go(ag(0, 1, k))
        go(ag(1, 1, k))
        go(sb(0, k))

    def arrive(h, k):
        for d in range(2):
            sg = 1 if d == 0 else -1
            ag(d, h, k).wait_recv()
            if h < H2:
                go(ag(d, h + 1, k))
                go(sb(-sg * h, k))
        if h == H2:
            go(sb(H2, k))

    def prep():
        gb = jnp.broadcast_to(gain_ref[...], (128, D)).T
        gainb[...] = gb.reshape(gainb.shape)
        wcp[0].wait()
        for j in range(FH // 128):
            t = wu[:, pl.ds(j * 128, 128)].astype(F32) * gb
            wg[:, pl.ds(j * 128, 128)] = t.astype(BF16)
            wgT[pl.ds(j * 128, 128), :] = t.T.astype(BF16)
        wcp[1].wait()

    def compute(k):
        for j in range(Y):
            sb(j, k).wait_recv()
        last = k == NCH - 1
        xc = B[k, :, 0:FB, :].reshape(D, TC)
        dc = B[k, :, FB : 2 * FB, :].reshape(D, TC)
        xf = xc.astype(F32)
        inv = lax.rsqrt(jnp.sum(xf * xf, axis=0, keepdims=True) * (1.0 / D) + EPSILON)
        live = live_s[k]
        v = nn_dot(wgT[...], xc) * inv
        a = nn_dot(wd[...], dc)
        v2 = v * v
        t = jnp.tanh(GC * v * (1.0 + 0.044715 * v2))
        cdf = 0.5 + 0.5 * t
        act = (v * cdf * live).astype(BF16)
        gp = cdf + (0.5 * GC) * v * (1.0 - t * t) * (1.0 + (3 * 0.044715) * v2)
        dh = a * gp * (live * inv)
        ct = jnp.sum(dh * v, axis=0, keepdims=True) * inv * (1.0 / D)
        dhb = dh.astype(BF16)

        def grads(u, lhs, rhs, acc):
            term = nt_dot(lhs, rhs)
            if k > 0:
                term = acc[...] + term
            acc[...] = term
            if last:
                Gs[u] = term.astype(BF16).reshape(Gs.shape[1:])
                for i in range(1, X):
                    go(xstage(u, i))

        grads(0, xc, dhb, U)
        if last:
            wuu = (wu[...].astype(F32) * U[...]).astype(BF16)
            gv = nt_dot(jnp.ones((8, FH), BF16), wuu)
            for j in range(Y):
                g1[j] = gv[:, j * 128 : (j + 1) * 128]
            go(gacopy())
        grads(1, dc, act, V)
        q = nn_dot(wg[...], dhb) - B[k, :, 0:FB, :].reshape(D, TC).astype(F32) * ct
        q = q.astype(BF16)
        for j in range(2 * Y):
            Q[k, j % 2, j // 2] = q[j * FB : (j + 1) * FB, :]
        go(qcopy(k))

    def qcopy(k):
        return remote(Q.at[k, 1 - c], Qs.at[k], qs_s.at[k], qs_r.at[k], sib)

    def gacopy():
        return remote(g1, g1r, ga_s, ga_r, sib)

    def xstage(u, i):
        return remote(
            Gs.at[u, (x + i) % X], Xr.at[u, i - 1], x_s.at[u, i - 1], x_r.at[u, i - 1], xdev(i)
        )

    def zstage(u, i):
        return remote(
            Ss.at[u, (z + i) % Z], Zr.at[u, i - 1], z_s.at[u, i - 1], z_r.at[u, i - 1], zdev(i)
        )

    def rs(d, h, k):
        sg = 1 if d == 0 else -1
        if h < H2:
            src, dst = RSs.at[d, h - 1, k], RSr.at[d, h - 1, k]
        else:
            src = RSs.at[d, h - 1, k, pl.ds(0, FB // 2)]
            dst = RSr.at[d, h - 1, k, pl.ds(0, FB // 2)]
        return remote(src, dst, rs_s.at[d, h - 1, k], rs_r.at[d, h - 1, k], ydev(sg))

    def came(d, h, k):
        rs(d, h, k).wait_recv()
        if h < H2:
            return RSr[d, h - 1, k].astype(F32)
        half = RSr[d, h - 1, k, 0 : FB // 2, :].astype(F32)
        zero = jnp.zeros_like(half)
        return jnp.concatenate([half, zero] if d == 0 else [zero, half], axis=0)

    def both(ty, k):
        return Q[k, c, ty].astype(F32) + Qs[k, ty].astype(F32)

    def rs_step(h, k):
        if h == H2:
            qcopy(k).wait_recv()
            p = both((y + H2) % Y, k).astype(BF16)
            RSs[0, h - 1, k, 0 : FB // 2, :] = p[0 : FB // 2, :]
            RSs[1, h - 1, k, 0 : FB // 2, :] = p[FB // 2 :, :]
            for d in range(2):
                go(rs(d, h, k))
            return
        for d in range(2):
            sg = 1 if d == 0 else -1
            p = both((y + sg * h + Y) % Y, k) + came(d, h + 1, k)
            RSs[d, h - 1, k] = p.astype(BF16)
            go(rs(d, h, k))

    def rs_end(k):
        tot = both(y, k) + came(0, 1, k) + came(1, 1, k)
        tot = B[k, m, FB : 2 * FB, :].astype(F32) + tot
        dtok_ref[:, pl.ds(k * TC, TC)] = (tot * live_s[k]).astype(BF16)

    def gain_a():
        gacopy().wait_recv()
        g2[...] = g1[...] + g1r[...]
        for i in range(1, Y):
            go(gycopy(i))

    def gycopy(i):
        return remote(g2.at[(y + i) % Y], gy.at[i - 1], gy_s.at[i - 1], gy_r.at[i - 1], ydev(i))

    def gxcopy(i):
        return remote(g3, gx.at[i - 1], gx_s.at[i - 1], gx_r.at[i - 1], xdev(i))

    def gzcopy(i):
        return remote(g4, gz.at[i - 1], gz_s.at[i - 1], gz_r.at[i - 1], zdev(i))

    def gain_x():
        t = g2[y]
        for i in range(1, Y):
            gycopy(i).wait_recv()
            t = t + gy[i - 1]
        g3[...] = t
        for i in range(1, X):
            go(gxcopy(i))

    def gain_z():
        t = g3[...]
        for i in range(1, X):
            gxcopy(i).wait_recv()
            t = t + gx[i - 1]
        g4[...] = t
        for i in range(1, Z):
            go(gzcopy(i))

    def gain_end():
        t = g4[...]
        for i in range(1, Z):
            gzcopy(i).wait_recv()
            t = t + gz[i - 1]
        t = t * s
        dgain_ref[...] = jnp.where(c == 0, t[0:1, 0:FB], t[0:1, FB : 2 * FB])

    def x_end(u):
        t = Gs[u, x].astype(F32)
        for i in range(1, X):
            xstage(u, i).wait_recv()
            t = t + Xr[u, i - 1].astype(F32)
        Ss[u] = t.astype(BF16)
        for i in range(1, Z):
            go(zstage(u, i))

    def z_end(u):
        t = Ss[u, z].astype(F32)
        for i in range(1, Z):
            zstage(u, i).wait_recv()
            t = t + Zr[u, i - 1].astype(F32)
        t = t * s
        if u == 0:
            gb = gainb[r]
            for j in range(FH // 128):
                dup_ref[:, pl.ds(j * 128, 128)] = t[:, j * 128 : (j + 1) * 128] * gb
        else:
            ddn_ref[...] = t

    own_send(0)
    own_send(1)
    prep()
    order = sorted(
        [(h + k, -h, h, k) for h in range(1, H2 + 1) for k in range(NCH)]
    )
    ready = []
    for at, (_, _, h, k) in enumerate(order):
        arrive(h, k)
        if h == 1 and k + 2 < NCH:
            own_send(k + 2)
        if ready:
            compute(ready.pop(0))
        if h == H2:
            ready.append(k)
    for k in ready:
        compute(k)

    steps = sorted([(H2 - h + k, h, k) for h in range(1, H2 + 1) for k in range(NCH)])
    extra = {2: [gain_a], 5: [gain_x], 8: [gain_z, lambda: x_end(0)], 12: [lambda: x_end(1)]}
    for at, (_, h, k) in enumerate(steps):
        rs_step(h, k)
        for f in extra.get(at, []):
            f()
    if len(steps) < 13:
        for at in sorted(extra):
            if at >= len(steps):
                for f in extra[at]:
                    f()
    for k in range(NCH):
        rs_end(k)
    gain_end()
    z_end(0)
    z_end(1)
    for cp in pending:
        cp.wait_send()


def solution(mesh):
    R, M = mesh.shape["region"], mesh.shape["mp"]
    X = max(k for k in (1, 2, 4) if k * k <= R)
    Z, Y = R // X, M // 2
    s = 1.0 / math.sqrt(BAL * R)

    def on_device(tokens, cotangent, gain, w_up, w_down, counts):
        T, FB = tokens.shape
        D, FH = w_up.shape
        TC = T // NCH
        RW = D // R
        H2 = Y // 2
        dma = pltpu.SemaphoreType.DMA
        scratch = [
            pltpu.VMEM((NCH, M, 2 * FB, TC), BF16),
            pltpu.VMEM((D, FH), BF16),
            pltpu.VMEM((FH, D), BF16),
            pltpu.VMEM((D, FH), BF16),
            pltpu.VMEM((FH, D), BF16),
            pltpu.VMEM((R, RW, 128), F32),
            pltpu.VMEM((NCH, 2, Y, FB, TC), BF16),
            pltpu.VMEM((NCH, Y, FB, TC), BF16),
            pltpu.VMEM((2, H2, NCH, FB, TC), BF16),
            pltpu.VMEM((2, H2, NCH, FB, TC), BF16),
            pltpu.VMEM((D, FH), F32),
            pltpu.VMEM((D, FH), F32),
            pltpu.VMEM((2, X, Z, RW, FH), BF16),
            pltpu.VMEM((2, X, Z, RW, FH), BF16),
            pltpu.VMEM((2, Z, RW, FH), BF16),
            pltpu.VMEM((2, Z, RW, FH), BF16),
            pltpu.VMEM((Y, 8, 128), F32),
            pltpu.VMEM((Y, 8, 128), F32),
            pltpu.VMEM((Y, 8, 128), F32),
            pltpu.VMEM((Y, 8, 128), F32),
            pltpu.VMEM((8, 128), F32),
            pltpu.VMEM((X, 8, 128), F32),
            pltpu.VMEM((8, 128), F32),
            pltpu.VMEM((Z, 8, 128), F32),
            pltpu.VMEM((NCH, 1, TC), F32),
            dma((2 * NCH + 2,)),
            dma((2, H2, NCH)),
            dma((2, H2, NCH)),
            dma((Y, NCH)),
            dma((Y, NCH)),
            dma((NCH,)),
            dma((NCH,)),
            dma((2, H2, NCH)),
            dma((2, H2, NCH)),
            dma((2, X)),
            dma((2, X)),
            dma((2, Z)),
            dma((2, Z)),
            dma,
            dma,
            dma((Y,)),
            dma((Y,)),
            dma((X,)),
            dma((X,)),
            dma((Z,)),
            dma((Z,)),
        ]
        hbm = pl.BlockSpec(memory_space=pl.ANY)
        vm = pl.BlockSpec(memory_space=pltpu.VMEM)
        sm = pl.BlockSpec(memory_space=pltpu.SMEM)
        dtok, dup, ddn, dgain = pl.pallas_call(
            functools.partial(kernel, X, Z, Y, s),
            out_shape=[
                jax.ShapeDtypeStruct((FB, T), BF16),
                jax.ShapeDtypeStruct((RW, FH), F32),
                jax.ShapeDtypeStruct((RW, FH), F32),
                jax.ShapeDtypeStruct((1, FB), F32),
            ],
            in_specs=[hbm, hbm, vm, hbm, hbm, sm],
            out_specs=[vm, vm, vm, vm],
            scratch_shapes=scratch,
            compiler_params=pltpu.CompilerParams(
                collective_id=0, has_side_effects=True, vmem_limit_bytes=44 << 20
            ),
            cost_estimate=pl.CostEstimate(
                flops=10 * T * D * FH, bytes_accessed=4 << 20, transcendentals=T * FH
            ),
        )(tokens.T, cotangent.T, gain.reshape(1, D), w_up, w_down, counts)
        return dtok.T, dup, ddn.T, dgain.reshape(FB)

    return jax.shard_map(
        on_device,
        mesh=mesh,
        in_specs=(
            P("region", "mp"), P("region", "mp"), P(), P(None, "mp"), P("mp", None), P("region"),
        ),
        out_specs=(P("region", "mp"), P("region", "mp"), P("mp", "region"), P("mp")),
        check_vma=False,
    )
```

time: 176 us -> 83.6 us (0.47)
  waiting for transfers between devices: 108 us -> 0 us
  Pallas kernels: 0 us -> 74.6 us
  starting transfers between devices: 29.6 us -> 0 us
  between operations: 13.9 us -> 0.66 us
  other arithmetic: 11.2 us -> 0 us
  matrix products: 9.63 us -> 0 us
  local copies, waits for them, and re-layouts: 3.7 us -> 6.96 us
    pallas_call x0 -> x1, Pallas kernels: none -> 74.6 us  [on_device(): pl.pallas_call(functools.partial(kernel, X, Z, Y, s), out_shape=[jax.Shap...]
    all_gather x1 -> x0, waiting for transfers between devices: 49.7 us -> none  [turned_gather(): whole = lax.all_gather(both, axis, axis=0, tiled=True)]
    reduce_scatter x2 -> x0, waiting for transfers between devices: 42.8 us -> none  [the longest x1 27.4 us: sum_by_chip(): return lax.psum_scatter(blocks, chips, scatter_dimension=0, tiled=True)[0]]
    all_to_all x3 -> x0, starting transfers between devices: 29.5 us -> none  [the longest x2 20.4 us: from_everyone(): lax.all_to_all(jnp.broadcast_to(value[None], (length, *value.shape)), axi...]
    all_to_all x3 -> x0, waiting for transfers between devices: 15 us -> none  [the longest x2 15 us: from_everyone(): lax.all_to_all(jnp.broadcast_to(value[None], (length, *value.shape)), axi...]
    dot_general x5 -> x0, matrix products: 9.63 us -> none  [the longest x1 2.74 us: backward(): hidden = jnp.dot(normed, w_up, preferred_element_type=jnp.float32)]
    unnamed x12 -> x16, local copies, waits for them, and re-layouts: 0.22 us -> 6.96 us
    reduce_sum x6 -> x0, other arithmetic: 5.23 us -> none  [the longest x1 2.07 us: backward(): inv_rms = lax.rsqrt(jnp.mean(whole_float * whole_float, axis=1) + EPSILON)]
  transfers between devices with their start and end apart: 6 -> 0, of which waited for: 5 -> 0; matrix products, arithmetic and copies ran while one was open for 6% -> 0% of each run, Pallas kernels for 0% -> 0%
where the time goes in v1:
time: 83.6 us; the launch traced here: 82.2 us
  Pallas kernels  74.6 us (89%)
  local copies, waits for them, and re-layouts  6.96 us (8%)
    pallas_call x1, Pallas kernels, on_device(): pl.pallas_call(functools.partial(kernel, X, Z, Y, s), out_shape=[jax.Shap...  74.6 us
    unnamed x16, local copies, waits for them, and re-layouts  6.96 us

profile of v1, /device:TPU:1, one launch (start us, length us, event | category | flops | bytes accessed | tf_op | source)
XLA Modules:
  0.0 82.2 jit_solution(210557163367566353)
XLA Ops:
  0.6 0.0 copy-start.4
  0.6 0.0 copy-start.5
  0.7 0.7 copy-done.4
  1.3 0.0 copy-done.5
  1.3 0.0 copy-start
  1.3 1.0 %copy-done = bf16[1024,256]{1,0:T(8,128)(2,1)S(1)} copy-done((bf16[1024,256]{1,0:T(8,128)(2,1)S(1)}, bf16[1024,256]{1,0:T(8,128)(2,1)}, u32[]{:S(2)}) %copy-start) | copy-done | bytes 524312
  2.4 0.0 copy-start.1
  2.4 1.0 %copy-done.1 = bf16[256,1024]{1,0:T(8,128)(2,1)S(1)} copy-done((bf16[256,1024]{1,0:T(8,128)(2,1)S(1)}, bf16[256,1024]{1,0:T(8,128)(2,1)}, u32[]{:S(2)}) %copy-start.1) | copy-done | bytes 524312
  3.4 0.0 copy-start.2
  3.4 0.9 %copy-done.2 = bf16[1024,64]{0,1:T(8,128)(2,1)S(1)} copy-done((bf16[1024,64]{0,1:T(8,128)(2,1)S(1)}, bf16[1024,64]{0,1:T(8,128)(2,1)}, u32[]{:S(2)}) %copy-start.2) | copy-done | bytes 131096
  4.3 0.0 copy-start.3
  4.3 0.9 %copy-done.3 = bf16[1024,64]{0,1:T(8,128)(2,1)S(1)} copy-done((bf16[1024,64]{0,1:T(8,128)(2,1)S(1)}, bf16[1024,64]{0,1:T(8,128)(2,1)}, u32[]{:S(2)}) %copy-start.3) | copy-done | bytes 131096
  5.2 74.6 %shard_map.93 = (bf16[64,1024]{1,0:T(8,128)(2,1)S(1)}, f32[32,256]{1,0:T(8,128)S(1)}, f32[32,256]{1,0:T(8,128)S(1)}, f32[1,64]{1,0:T(1,128)S(1)}) custom-call(bf16[64,1024]{1,0:T(8,128)(2,1)S(1)} %bitcast.8, bf16[64,1024]{1,0:T(8,128)(2,1)S(1)} %bitcast.9, f32[1,1024]{1,0:T(1,128)S(1)} %bitcast.10, bf16[1024,256]{1,0:T(8,128)(2,1)S(1)} %copy-done, ...), custom_call_target="tpu_custom_call" | custom-call | flops 2684354560 | bytes 4194304 | tf_op jit(solution)/shard_map/pallas_call | solution.py:393
  79.8 0.7 copy.14
  80.5 0.6 copy.15
  81.1 0.6 copy.16
  81.7 0.5 copy.17
Async XLA Ops:
  0.6 0.7 copy-start.4
  0.6 0.7 copy-start.5
  1.3 1.0 %copy-start = (bf16[1024,256]{1,0:T(8,128)(2,1)S(1)}, bf16[1024,256]{1,0:T(8,128)(2,1)}, u32[]{:S(2)}) copy-start(bf16[1024,256]{1,0:T(8,128)(2,1)} %wu_hbm.1) | copy-start | bytes 1572868
  2.4 1.0 %copy-start.1 = (bf16[256,1024]{1,0:T(8,128)(2,1)S(1)}, bf16[256,1024]{1,0:T(8,128)(2,1)}, u32[]{:S(2)}) copy-start(bf16[256,1024]{1,0:T(8,128)(2,1)} %wd_hbm.1) | copy-start | bytes 1572868
  3.4 0.9 %copy-start.2 = (bf16[1024,64]{0,1:T(8,128)(2,1)S(1)}, bf16[1024,64]{0,1:T(8,128)(2,1)}, u32[]{:S(2)}) copy-start(bf16[1024,64]{0,1:T(8,128)(2,1)} %param.6) | copy-start | bytes 393220
  4.3 0.9 %copy-start.3 = (bf16[1024,64]{0,1:T(8,128)(2,1)S(1)}, bf16[1024,64]{0,1:T(8,128)(2,1)}, u32[]{:S(2)}) copy-start(bf16[1024,64]{0,1:T(8,128)(2,1)} %param.7) | copy-start | bytes 393220

commit v2 on v1

--- a/solution.py
+++ b/solution.py
@@ -14,6 +14,8 @@
 F32 = jnp.float32
 BF16 = jnp.bfloat16
 NCH = 4
+ZFIRST = 1
+HF = 128
 GC = math.sqrt(2.0 / math.pi)
 
 
@@ -25,11 +27,30 @@
     return lax.dot_general(a, b, (((1,), (0,)), ((), ())), preferred_element_type=F32)
 
 
+def order_of(H2):
+    last = NCH - 1
+    seq = [("own", 0, k) for k in range(NCH)] + [("prep", 0, 0)]
+    seq += [("arrive", h, k) for h in range(1, H2) for k in range(NCH)]
+    for k in range(NCH):
+        seq.append(("arrive", H2, k))
+        if 1 <= k < last:
+            seq.append(("compute", 0, k - 1))
+    far = [("rs", H2, k) for k in range(NCH)]
+    near = [("rs", h, k) for h in range(H2 - 1, 0, -1) for k in range(NCH)]
+    seq += [far[0], ("compute", 0, last - 1), far[1], ("compute", 0, last)] + far[2:]
+    seq += near[:NCH] + [("gain_a", 0, 0)] + near[NCH : NCH + 2]
+    seq += [("first", 0, 0), ("drain", 0, 0)] + near[NCH + 2 : 2 * NCH] + [("gain_x", 0, 0)]
+    seq += [("first", 0, 1), ("first", 0, 2)] + near[2 * NCH :]
+    seq += [("gain_z", 0, 0), ("rs_end", 0, 0), ("rs_end", 0, 1), ("first", 0, 3)]
+    seq += [("rs_end", 0, k) for k in range(2, NCH)] + [("second", 0, 0), ("second", 0, 2)]
+    return seq + [("gain_end", 0, 0), ("second", 0, 1), ("second", 0, 3)]
+
+
 def kernel(
     X, Z, Y, s,
-    x_hbm, d_hbm, gain_ref, wu_hbm, wd_hbm, counts_ref,
+    x_hbm, d_hbm, gain_hbm, wu_hbm, wd_hbm, counts_hbm,
     dtok_ref, dup_ref, ddn_ref, dgain_ref,
-    B, wu, wd, wg, wgT, gainb, Q, Qs, RSs, RSr, U, V, Gs, Xr, Ss, Zr,
+    counts_ref, gain_ref, B, wu, wd, wg, wgT, gainb, Q, Qs, RSs, RSr, U, V, Gs, Xr, Ss, Zr, Gz, Zf, Sx, Xf,
     g1, g1r, g2, gy, g3, gx, g4, gz, live_s,
     loc, ag_s, ag_r, sb_s, sb_r, qs_s, qs_r, rs_s, rs_r, x_s, x_r, z_s, z_r,
     ga_s, ga_r, gy_s, gy_r, gx_s, gx_r, gz_s, gz_r,
@@ -68,9 +89,12 @@
     wcp = [
         pltpu.make_async_copy(wu_hbm, wu, loc.at[2 * NCH]),
         pltpu.make_async_copy(wd_hbm, wd, loc.at[2 * NCH + 1]),
+        pltpu.make_async_copy(gain_hbm, gain_ref, loc.at[2 * NCH + 2]),
+        pltpu.make_async_copy(counts_hbm, counts_ref, loc.at[2 * NCH + 3]),
     ]
     for cp in own + wcp:
         cp.start()
+    wcp[3].wait()
     load = counts_ref[0] + counts_ref[1] + counts_ref[2] + counts_ref[3]
     for k in range(NCH):
         at = lax.broadcasted_iota(jnp.int32, (1, TC), 1) + k * TC
@@ -116,6 +140,7 @@
             go(sb(H2, k))
 
     def prep():
+        wcp[2].wait()
         gb = jnp.broadcast_to(gain_ref[...], (128, D)).T
         gainb[...] = gb.reshape(gainb.shape)
         wcp[0].wait()
@@ -151,9 +176,19 @@
                 term = acc[...] + term
             acc[...] = term
             if last:
-                Gs[u] = term.astype(BF16).reshape(Gs.shape[1:])
-                for i in range(1, X):
-                    go(xstage(u, i))
+                for p in (2 * u + 1, 2 * u):
+                    half = term[:, (p % 2) * HF : (p % 2) * HF + HF].astype(BF16)
+                    half = half.reshape(X, Z, -1, HF)
+                    if p == ZFIRST:
+                        for i in range(X):
+                            for j in range(Z):
+                                Gz[j, i] = half[i, j]
+                        for i in range(1, Z):
+                            go(z_first(i))
+                    else:
+                        Gs[p] = half
+                        for i in range(1, X):
+                            go(xstage(p, i))
 
         grads(0, xc, dhb, U)
         if last:
@@ -175,14 +210,26 @@
     def gacopy():
         return remote(g1, g1r, ga_s, ga_r, sib)
 
-    def xstage(u, i):
+    def xstage(p, i):
         return remote(
-            Gs.at[u, (x + i) % X], Xr.at[u, i - 1], x_s.at[u, i - 1], x_r.at[u, i - 1], xdev(i)
+            Gs.at[p, (x + i) % X], Xr.at[p, i - 1], x_s.at[p, i - 1], x_r.at[p, i - 1], xdev(i)
         )
 
-    def zstage(u, i):
+    def zstage(p, i):
         return remote(
-            Ss.at[u, (z + i) % Z], Zr.at[u, i - 1], z_s.at[u, i - 1], z_r.at[u, i - 1], zdev(i)
+            Ss.at[p, (z + i) % Z], Zr.at[p, i - 1], z_s.at[p, i - 1], z_r.at[p, i - 1], zdev(i)
+        )
+
+    def z_first(i):
+        p = ZFIRST
+        return remote(
+            Gz.at[(z + i) % Z], Zf.at[i - 1], z_s.at[p, i - 1], z_r.at[p, i - 1], zdev(i)
+        )
+
+    def x_second(i):
+        p = ZFIRST
+        return remote(
+            Sx.at[(x + i) % X], Xf.at[i - 1], x_s.at[p, i - 1], x_r.at[p, i - 1], xdev(i)
         )
 
     def rs(d, h, k):
@@ -266,64 +313,81 @@
         t = t * s
         dgain_ref[...] = jnp.where(c == 0, t[0:1, 0:FB], t[0:1, FB : 2 * FB])
 
-    def x_end(u):
-        t = Gs[u, x].astype(F32)
-        for i in range(1, X):
-            xstage(u, i).wait_recv()
-            t = t + Xr[u, i - 1].astype(F32)
-        Ss[u] = t.astype(BF16)
-        for i in range(1, Z):
-            go(zstage(u, i))
-
-    def z_end(u):
-        t = Ss[u, z].astype(F32)
-        for i in range(1, Z):
-            zstage(u, i).wait_recv()
-            t = t + Zr[u, i - 1].astype(F32)
+    def first_end(p):
+        if p == ZFIRST:
+            t = Gz[z].astype(F32)
+            for i in range(1, Z):
+                z_first(i).wait_recv()
+                t = t + Zf[i - 1].astype(F32)
+            Sx[...] = t.astype(BF16)
+            for i in range(1, X):
+                go(x_second(i))
+        else:
+            t = Gs[p, x].astype(F32)
+            for i in range(1, X):
+                xstage(p, i).wait_recv()
+                t = t + Xr[p, i - 1].astype(F32)
+            Ss[p] = t.astype(BF16)
+            for i in range(1, Z):
+                go(zstage(p, i))
+
+    def second_end(p):
+        if p == ZFIRST:
+            t = Sx[x].astype(F32)
+            for i in range(1, X):
+                x_second(i).wait_recv()
+                t = t + Xf[i - 1].astype(F32)
+        else:
+            t = Ss[p, z].astype(F32)
+            for i in range(1, Z):
+                zstage(p, i).wait_recv()
+                t = t + Zr[p, i - 1].astype(F32)
         t = t * s
-        if u == 0:
-            gb = gainb[r]
-            for j in range(FH // 128):
-                dup_ref[:, pl.ds(j * 128, 128)] = t[:, j * 128 : (j + 1) * 128] * gb
+        lanes = pl.ds((p % 2) * HF, HF)
+        if p < 2:
+            dup_ref[:, lanes] = t * gainb[r]
         else:
-            ddn_ref[...] = t
-
-    own_send(0)
-    own_send(1)
-    prep()
-    order = sorted(
-        [(h + k, -h, h, k) for h in range(1, H2 + 1) for k in range(NCH)]
-    )
-    ready = []
-    for at, (_, _, h, k) in enumerate(order):
-        arrive(h, k)
-        if h == 1 and k + 2 < NCH:
-            own_send(k + 2)
-        if ready:
-            compute(ready.pop(0))
-        if h == H2:
-            ready.append(k)
-    for k in ready:
-        compute(k)
-
-    steps = sorted([(H2 - h + k, h, k) for h in range(1, H2 + 1) for k in range(NCH)])
-    extra = {2: [gain_a], 5: [gain_x], 8: [gain_z, lambda: x_end(0)], 12: [lambda: x_end(1)]}
-    for at, (_, h, k) in enumerate(steps):
-        rs_step(h, k)
-        for f in extra.get(at, []):
-            f()
-    if len(steps) < 13:
-        for at in sorted(extra):
-            if at >= len(steps):
-                for f in extra[at]:
-                    f()
-    for k in range(NCH):
-        rs_end(k)
-    gain_end()
-    z_end(0)
-    z_end(1)
-    for cp in pending:
+            ddn_ref[:, lanes] = t
+
+    def drain():
+        for cp in pending[:drained]:
+            cp.wait_send()
+
+    steps = {
+        "own": lambda h, k: own_send(k),
+        "prep": lambda h, k: prep(),
+        "arrive": arrive,
+        "compute": lambda h, k: compute(k),
+        "rs": rs_step,
+        "rs_end": lambda h, k: rs_end(k),
+        "first": lambda h, k: first_end(k),
+        "second": lambda h, k: second_end(k),
+        "gain_a": lambda h, k: gain_a(),
+        "gain_x": lambda h, k: gain_x(),
+        "gain_z": lambda h, k: gain_z(),
+        "gain_end": lambda h, k: gain_end(),
+        "drain": lambda h, k: drain(),
+    }
+    for what, h, k in order_of(H2):
+        if what == "compute":
+            drained = len(pending) if k == 0 else drained
+        steps[what](h, k)
+    for cp in pending[drained:]:
         cp.wait_send()
+
+
+def hand_out(*refs):
+    n = (len(refs) - 2) // 3
+    into, out = refs[-2], refs[-1]
+    loads = [pltpu.make_async_copy(refs[i], refs[2 * n + i], into.at[i]) for i in range(n)]
+    stores = [pltpu.make_async_copy(refs[2 * n + i], refs[n + i], out.at[i]) for i in range(n)]
+    for cp in loads:
+        cp.start()
+    for cp, st in zip(loads, stores):
+        cp.wait()
+        st.start()
+    for st in stores:
+        st.wait()
 
 
 def solution(mesh):
@@ -340,6 +404,8 @@
         H2 = Y // 2
         dma = pltpu.SemaphoreType.DMA
         scratch = [
+            pltpu.SMEM((4,), jnp.int32),
+            pltpu.VMEM((1, D), F32),
             pltpu.VMEM((NCH, M, 2 * FB, TC), BF16),
             pltpu.VMEM((D, FH), BF16),
             pltpu.VMEM((FH, D), BF16),
@@ -352,10 +418,14 @@
             pltpu.VMEM((2, H2, NCH, FB, TC), BF16),
             pltpu.VMEM((D, FH), F32),
             pltpu.VMEM((D, FH), F32),
-            pltpu.VMEM((2, X, Z, RW, FH), BF16),
-            pltpu.VMEM((2, X, Z, RW, FH), BF16),
-            pltpu.VMEM((2, Z, RW, FH), BF16),
-            pltpu.VMEM((2, Z, RW, FH), BF16),
+            pltpu.VMEM((4, X, Z, RW, HF), BF16),
+            pltpu.VMEM((4, X, Z, RW, HF), BF16),
+            pltpu.VMEM((4, Z, RW, HF), BF16),
+            pltpu.VMEM((4, Z, RW, HF), BF16),
+            pltpu.VMEM((Z, X, RW, HF), BF16),
+            pltpu.VMEM((Z, X, RW, HF), BF16),
+            pltpu.VMEM((X, RW, HF), BF16),
+            pltpu.VMEM((X, RW, HF), BF16),
             pltpu.VMEM((Y, 8, 128), F32),
             pltpu.VMEM((Y, 8, 128), F32),
             pltpu.VMEM((Y, 8, 128), F32),
@@ -365,7 +435,7 @@
             pltpu.VMEM((8, 128), F32),
             pltpu.VMEM((Z, 8, 128), F32),
             pltpu.VMEM((NCH, 1, TC), F32),
-            dma((2 * NCH + 2,)),
+            dma((2 * NCH + 4,)),
             dma((2, H2, NCH)),
             dma((2, H2, NCH)),
             dma((Y, NCH)),
@@ -374,10 +444,10 @@
             dma((NCH,)),
             dma((2, H2, NCH)),
             dma((2, H2, NCH)),
-            dma((2, X)),
-            dma((2, X)),
-            dma((2, Z)),
-            dma((2, Z)),
+            dma((4, X)),
+            dma((4, X)),
+            dma((4, Z)),
+            dma((4, Z)),
             dma,
             dma,
             dma((Y,)),
@@ -387,27 +457,35 @@
             dma((Z,)),
             dma((Z,)),
         ]
-        hbm = pl.BlockSpec(memory_space=pl.ANY)
+        hbm = pl.BlockSpec(memory_space=pltpu.HBM)
         vm = pl.BlockSpec(memory_space=pltpu.VMEM)
-        sm = pl.BlockSpec(memory_space=pltpu.SMEM)
-        dtok, dup, ddn, dgain = pl.pallas_call(
+        shapes = [
+            jax.ShapeDtypeStruct((FB, T), BF16),
+            jax.ShapeDtypeStruct((RW, FH), F32),
+            jax.ShapeDtypeStruct((RW, FH), F32),
+            jax.ShapeDtypeStruct((1, FB), F32),
+        ]
+        sums = pl.pallas_call(
             functools.partial(kernel, X, Z, Y, s),
-            out_shape=[
-                jax.ShapeDtypeStruct((FB, T), BF16),
-                jax.ShapeDtypeStruct((RW, FH), F32),
-                jax.ShapeDtypeStruct((RW, FH), F32),
-                jax.ShapeDtypeStruct((1, FB), F32),
-            ],
-            in_specs=[hbm, hbm, vm, hbm, hbm, sm],
+            out_shape=shapes,
+            in_specs=[hbm] * 6,
             out_specs=[vm, vm, vm, vm],
             scratch_shapes=scratch,
             compiler_params=pltpu.CompilerParams(
-                collective_id=0, has_side_effects=True, vmem_limit_bytes=44 << 20
+                collective_id=0, has_side_effects=True, vmem_limit_bytes=56 << 20
             ),
             cost_estimate=pl.CostEstimate(
                 flops=10 * T * D * FH, bytes_accessed=4 << 20, transcendentals=T * FH
             ),
         )(tokens.T, cotangent.T, gain.reshape(1, D), w_up, w_down, counts)
+        dtok, dup, ddn, dgain = pl.pallas_call(
+            hand_out,
+            out_shape=shapes,
+            in_specs=[hbm] * 4,
+            out_specs=[hbm] * 4,
+            scratch_shapes=[pltpu.VMEM(t.shape, t.dtype) for t in shapes] + [dma((4,)), dma((4,))],
+            compiler_params=pltpu.CompilerParams(vmem_limit_bytes=56 << 20),
+        )(*sums)
         return dtok.T, dup, ddn.T, dgain.reshape(FB)
 
     return jax.shard_map(

time: 83.6 us -> 66.5 us (0.80); the launches traced: 82.2 us -> 66.2 us
  Pallas kernels: 74.6 us -> 65.6 us
  local copies, waits for them, and re-layouts: 6.96 us -> 0 us
    pallas_call x1 -> x2, Pallas kernels: 74.6 us -> 65.6 us  [the longest x1 63.9 us: on_device(): pl.pallas_call(functools.partial(kernel, X, Z, Y, s), out_shape=shapes, i...]
    unnamed x16 -> x0, local copies, waits for them, and re-layouts: 6.96 us -> none
where the time goes in v2:
time: 66.5 us; the launch traced here: 66.2 us
  Pallas kernels  65.6 us (99%)
    pallas_call x1, Pallas kernels, on_device(): pl.pallas_call(functools.partial(kernel, X, Z, Y, s), out_shape=shapes, i...  63.9 us
    pallas_call x1, Pallas kernels, on_device(): pl.pallas_call(hand_out, out_shape=shapes, in_specs=[hbm] * 4, out_specs=...  1.64 us

profile of v2, /device:TPU:1, one launch (start us, length us, event | category | flops | bytes accessed | tf_op | source)
XLA Modules:
  0.0 66.2 jit_solution(2284593198676665538)
XLA Ops:
  0.6 63.9 %shard_map.93 = (bf16[64,1024]{1,0:T(8,128)(2,1)}, f32[32,256]{1,0:T(8,128)}, f32[32,256]{1,0:T(8,128)}, f32[1,64]{1,0:T(1,128)}) custom-call(bf16[64,1024]{1,0:T(8,128)(2,1)} %bitcast.6, bf16[64,1024]{1,0:T(8,128)(2,1)} %bitcast.7, f32[1,1024]{1,0:T(1,128)} %bitcast.10, bf16[1024,256]{1,0:T(8,128)(2,1)} %wu_hbm.1, bf16[256,1024]{1,0:T(8,128)(2,1)} %wd_hbm.1, ...), custom_call_target="tpu_custom_call" | custom-call | flops 2684354560 | bytes 4194304 | tf_op jit(solution)/shard_map/pallas_call | solution.py:468
  64.6 1.6 %shard_map.94 = (bf16[64,1024]{1,0:T(8,128)(2,1)}, f32[32,256]{1,0:T(8,128)}, f32[32,256]{1,0:T(8,128)}, f32[1,64]{1,0:T(1,128)}) custom-call(bf16[64,1024]{1,0:T(8,128)(2,1)} %get-tuple-element.12.refs_0_, f32[32,256]{1,0:T(8,128)} %get-tuple-element.13.refs_1_, f32[32,256]{1,0:T(8,128)} %get-tuple-element.14.refs_2_, f32[1,64]{1,0:T(1,128)} %get-tuple-element.15.refs_3_), custom_call_target="tpu_custom_call" | custom-call | tf_op jit(solution)/shard_map/pallas_call | solution.py:481

commit v3 on v2

--- a/solution.py
+++ b/solution.py
@@ -30,20 +30,21 @@
 def order_of(H2):
     last = NCH - 1
     seq = [("own", 0, k) for k in range(NCH)] + [("prep", 0, 0)]
-    seq += [("arrive", h, k) for h in range(1, H2) for k in range(NCH)]
+    for h in range(1, H2):
+        seq += [("tell", h, 0)] + [("arrive", h, k) for k in range(NCH)]
     for k in range(NCH):
         seq.append(("arrive", H2, k))
         if 1 <= k < last:
             seq.append(("compute", 0, k - 1))
-    far = [("rs", H2, k) for k in range(NCH)]
-    near = [("rs", h, k) for h in range(H2 - 1, 0, -1) for k in range(NCH)]
-    seq += [far[0], ("compute", 0, last - 1), far[1], ("compute", 0, last)] + far[2:]
-    seq += near[:NCH] + [("gain_a", 0, 0)] + near[NCH : NCH + 2]
-    seq += [("first", 0, 0), ("drain", 0, 0)] + near[NCH + 2 : 2 * NCH] + [("gain_x", 0, 0)]
-    seq += [("first", 0, 1), ("first", 0, 2)] + near[2 * NCH :]
-    seq += [("gain_z", 0, 0), ("rs_end", 0, 0), ("rs_end", 0, 1), ("first", 0, 3)]
-    seq += [("rs_end", 0, k) for k in range(2, NCH)] + [("second", 0, 0), ("second", 0, 2)]
-    return seq + [("gain_end", 0, 0), ("second", 0, 1), ("second", 0, 3)]
+    far = [[("rs", H2, k), ("rs", H2 - 1, k)] for k in range(NCH)]
+    near = [("rs", h, k) for h in range(H2 - 2, 0, -1) for k in range(NCH)]
+    seq += far[0] + [("compute", 0, last - 1)] + far[1] + [("compute", 0, last)]
+    seq += [near[0]] + far[2] + [near[1]] + far[3] + [("gain_a", 0, 0), ("drain", 0, 0)]
+    seq += [near[2], ("first", 0, 0), near[4], near[3], near[5], ("gain_x", 0, 0)]
+    seq += [near[6], ("first", 0, 3), ("first", 0, 1), near[7]]
+    seq += [("rs_end", 0, 0), ("rs_end", 0, 1), ("gain_z", 0, 0), ("rs_end", 0, 2), ("first", 0, 2)]
+    seq += [("rs_end", 0, 3), ("second", 0, 0), ("second", 0, 3)]
+    return seq + [("gain_end", 0, 0), ("second", 0, 1), ("second", 0, 2)]
 
 
 def kernel(
@@ -53,7 +54,7 @@
     counts_ref, gain_ref, B, wu, wd, wg, wgT, gainb, Q, Qs, RSs, RSr, U, V, Gs, Xr, Ss, Zr, Gz, Zf, Sx, Xf,
     g1, g1r, g2, gy, g3, gx, g4, gz, live_s,
     loc, ag_s, ag_r, sb_s, sb_r, qs_s, qs_r, rs_s, rs_r, x_s, x_r, z_s, z_r,
-    ga_s, ga_r, gy_s, gy_r, gx_s, gx_r, gz_s, gz_r,
+    ga_s, ga_r, gy_s, gy_r, gx_s, gx_r, gz_s, gz_r, told,
 ):
     r = lax.axis_index("region")
     m = lax.axis_index("mp")
@@ -70,14 +71,15 @@
         return (r, ((y + k + Y) % Y) * 2 + c)
 
     def xdev(k):
-        return (((x + k) % X) * Z + z, m)
+        return (((x + k + X) % X) * Z + z, m)
 
     def zdev(k):
-        return (x * Z + (z + k) % Z, m)
+        return (x * Z + (z + k + Z) % Z, m)
 
     bar = pltpu.get_barrier_semaphore()
-    peers = [sib] + [ydev(k) for k in range(1, Y)] + [xdev(k) for k in range(1, X)]
-    peers += [zdev(k) for k in range(1, Z)]
+    sides = [(ydev(1), 1, H2), (ydev(-1), 0, H2), (zdev(1), 3, Z // 2), (zdev(-1), 2, Z // 2)]
+    sides += [(xdev(1), 5, X // 2), (xdev(-1), 4, X // 2)]
+    peers = [sib] + [p for p, _, _ in sides]
     for p in peers:
         pl.semaphore_signal(bar, 1, device_id=p, device_id_type=MESH)
 
@@ -105,6 +107,13 @@
 
     pending = []
 
+    def tell(n):
+        at = [i for i in range(6) if sides[i][2] > n]
+        for i in at:
+            pl.semaphore_signal(told.at[sides[i][1]], 1, device_id=sides[i][0], device_id_type=MESH)
+        for i in at:
+            pl.semaphore_wait(told.at[i], 1)
+
     def remote(src, dst, ss, rs, dev):
         return pltpu.make_async_remote_copy(
             src_ref=src, dst_ref=dst, send_sem=ss, recv_sem=rs, device_id=dev, device_id_type=MESH
@@ -237,6 +246,7 @@
         if h < H2:
             src, dst = RSs.at[d, h - 1, k], RSr.at[d, h - 1, k]
         else:
+            sg = 2 * sg
             src = RSs.at[d, h - 1, k, pl.ds(0, FB // 2)]
             dst = RSr.at[d, h - 1, k, pl.ds(0, FB // 2)]
         return remote(src, dst, rs_s.at[d, h - 1, k], rs_r.at[d, h - 1, k], ydev(sg))
@@ -263,7 +273,11 @@
             return
         for d in range(2):
             sg = 1 if d == 0 else -1
-            p = both((y + sg * h + Y) % Y, k) + came(d, h + 1, k)
+            p = both((y + sg * h + Y) % Y, k)
+            if h < H2 - 1:
+                p = p + came(d, h + 1, k)
+            if h == H2 - 2:
+                p = p + came(d, H2, k)
             RSs[d, h - 1, k] = p.astype(BF16)
             go(rs(d, h, k))
 
@@ -367,6 +381,7 @@
         "gain_z": lambda h, k: gain_z(),
         "gain_end": lambda h, k: gain_end(),
         "drain": lambda h, k: drain(),
+        "tell": lambda h, k: tell(h),
     }
     for what, h, k in order_of(H2):
         if what == "compute":
@@ -456,6 +471,7 @@
             dma((X,)),
             dma((Z,)),
             dma((Z,)),
+            pltpu.SemaphoreType.REGULAR((6,)),
         ]
         hbm = pl.BlockSpec(memory_space=pltpu.HBM)
         vm = pl.BlockSpec(memory_space=pltpu.VMEM)

time: 66.5 us -> 64 us (0.962)
  the two profiles are of different devices: /device:TPU:1 before, /device:TPU:64 now
where the time goes in v3:
time: 64 us; the launch traced here: 63.9 us
  Pallas kernels  63.2 us (99%)
  between operations  0.64 us (1%)
    pallas_call x1, Pallas kernels, on_device(): pl.pallas_call(functools.partial(kernel, X, Z, Y, s), out_shape=shapes, i...  61.6 us
    pallas_call x1, Pallas kernels, on_device(): pl.pallas_call(hand_out, out_shape=shapes, in_specs=[hbm] * 4, out_specs=...  1.64 us

profile of v3, /device:TPU:64, one launch (start us, length us, event | category | flops | bytes accessed | tf_op | source)
XLA Modules:
  0.0 63.9 jit_solution(13802922327899235089)
XLA Ops:
  0.6 61.6 %shard_map.93 = (bf16[64,1024]{1,0:T(8,128)(2,1)}, f32[32,256]{1,0:T(8,128)}, f32[32,256]{1,0:T(8,128)}, f32[1,64]{1,0:T(1,128)}) custom-call(bf16[64,1024]{1,0:T(8,128)(2,1)} %bitcast.6, bf16[64,1024]{1,0:T(8,128)(2,1)} %bitcast.7, f32[1,1024]{1,0:T(1,128)} %bitcast.10, bf16[1024,256]{1,0:T(8,128)(2,1)} %wu_hbm.1, bf16[256,1024]{1,0:T(8,128)(2,1)} %wd_hbm.1, ...), custom_call_target="tpu_custom_call" | custom-call | flops 2684354560 | bytes 4194304 | tf_op jit(solution)/shard_map/pallas_call | solution.py:484
  62.2 1.6 %shard_map.94 = (bf16[64,1024]{1,0:T(8,128)(2,1)}, f32[32,256]{1,0:T(8,128)}, f32[32,256]{1,0:T(8,128)}, f32[1,64]{1,0:T(1,128)}) custom-call(bf16[64,1024]{1,0:T(8,128)(2,1)} %get-tuple-element.12.refs_0_, f32[32,256]{1,0:T(8,128)} %get-tuple-element.13.refs_1_, f32[32,256]{1,0:T(8,128)} %get-tuple-element.14.refs_2_, f32[1,64]{1,0:T(1,128)} %get-tuple-element.15.refs_3_), custom_call_target="tpu_custom_call" | custom-call | tf_op jit(solution)/shard_map/pallas_call | solution.py:497

commit v4 on v3

--- a/solution.py
+++ b/solution.py
@@ -14,7 +14,7 @@
 F32 = jnp.float32
 BF16 = jnp.bfloat16
 NCH = 4
-ZFIRST = 1
+ZFIRST = (1,)
 HF = 128
 GC = math.sqrt(2.0 / math.pi)
 
@@ -31,29 +31,36 @@
     last = NCH - 1
     seq = [("own", 0, k) for k in range(NCH)] + [("prep", 0, 0)]
     for h in range(1, H2):
-        seq += [("tell", h, 0)] + [("arrive", h, k) for k in range(NCH)]
+        seq += [("tell", h - 1, 0)] if h > 1 else []
+        seq += [("arrive", h, k) for k in range(NCH)]
+    seq.append(("tell", H2 - 1, 0))
     for k in range(NCH):
         seq.append(("arrive", H2, k))
         if 1 <= k < last:
             seq.append(("compute", 0, k - 1))
+    seq.append(("hear", H2 - 1, 0))
     far = [[("rs", H2, k), ("rs", H2 - 1, k)] for k in range(NCH)]
     near = [("rs", h, k) for h in range(H2 - 2, 0, -1) for k in range(NCH)]
-    seq += far[0] + [("compute", 0, last - 1)] + far[1] + [("compute", 0, last)]
-    seq += [near[0]] + far[2] + [near[1]] + far[3] + [("gain_a", 0, 0), ("drain", 0, 0)]
-    seq += [near[2], ("first", 0, 0), near[4], near[3], near[5], ("gain_x", 0, 0)]
-    seq += [near[6], ("first", 0, 3), ("first", 0, 1), near[7]]
-    seq += [("rs_end", 0, 0), ("rs_end", 0, 1), ("gain_z", 0, 0), ("rs_end", 0, 2), ("first", 0, 2)]
-    seq += [("rs_end", 0, 3), ("second", 0, 0), ("second", 0, 3)]
-    return seq + [("gain_end", 0, 0), ("second", 0, 1), ("second", 0, 2)]
+    term = [("terms", 0, k) for k in range(NCH)]
+    one = {p: ("first", 0, p) for p in range(4)}
+    two = {p: ("second", 0, p) for p in range(4)}
+    seq += [("compute", 0, last - 1), ("compute", 0, last), ("gain", 0, 0)]
+    seq += [term[0], ("gain_a", 0, 0), term[1]] + far[0] + [term[2]] + far[1]
+    seq += [one[0], ("calm", 0, 0), ("gain_x", 0, 0), term[3]] + far[2] + far[3]
+    seq += [one[3], near[0], one[1], near[1], ("gain_z", 0, 0), near[2], one[2], near[3]]
+    seq += near[4:] + [("rs_end", 0, k) for k in range(NCH)]
+    seq += [two[0], two[3], ("gain_end", 0, 0), ("drain", 0, 0), two[1], two[2]]
+    return seq
 
 
 def kernel(
     X, Z, Y, s,
     x_hbm, d_hbm, gain_hbm, wu_hbm, wd_hbm, counts_hbm,
+    dtok_out, dup_out, ddn_out, dgain_out,
     dtok_ref, dup_ref, ddn_ref, dgain_ref,
     counts_ref, gain_ref, B, wu, wd, wg, wgT, gainb, Q, Qs, RSs, RSr, U, V, Gs, Xr, Ss, Zr, Gz, Zf, Sx, Xf,
-    g1, g1r, g2, gy, g3, gx, g4, gz, live_s,
-    loc, ag_s, ag_r, sb_s, sb_r, qs_s, qs_r, rs_s, rs_r, x_s, x_r, z_s, z_r,
+    DH, CT, g1, g1r, g2, gy, g3, gx, g4, gz, live_s,
+    loc, out_s, ag_s, ag_r, sb_s, sb_r, qs_s, qs_r, rs_s, rs_r, x_s, x_r, z_s, z_r,
     ga_s, ga_r, gy_s, gy_r, gx_s, gx_r, gz_s, gz_r, told,
 ):
     r = lax.axis_index("region")
@@ -79,9 +86,14 @@
     bar = pltpu.get_barrier_semaphore()
     sides = [(ydev(1), 1, H2), (ydev(-1), 0, H2), (zdev(1), 3, Z // 2), (zdev(-1), 2, Z // 2)]
     sides += [(xdev(1), 5, X // 2), (xdev(-1), 4, X // 2)]
-    peers = [sib] + [p for p, _, _ in sides]
-    for p in peers:
+
+    def greet(p):
         pl.semaphore_signal(bar, 1, device_id=p, device_id_type=MESH)
+
+    for p in [sib, ydev(1), ydev(-1), xdev(1), xdev(-1)]:
+        greet(p)
+    pl.when(z < Z - 1)(lambda: greet(zdev(1)))
+    pl.when(z > 0)(lambda: greet(zdev(-1)))
 
     own = []
     for k in range(NCH):
@@ -103,16 +115,32 @@
         live_s[k] = jnp.where(at < load, 1.0, 0.0).astype(F32)
     for cp in own:
         cp.wait()
-    pl.semaphore_wait(bar, len(peers))
+    pl.when(z == 0)(lambda: pl.semaphore_wait(bar, 6))
+    pl.when(z > 0)(lambda: pl.semaphore_wait(bar, 7))
+    pl.when(z == 0)(lambda: greet(zdev(-1)))
+    pl.when(z == Z - 1)(lambda: greet(zdev(1)))
 
     pending = []
 
+    def hear(n):
+        for i in range(6):
+            if sides[i][2] > n > 0:
+                pl.semaphore_wait(told.at[i], 1)
+
     def tell(n):
-        at = [i for i in range(6) if sides[i][2] > n]
-        for i in at:
-            pl.semaphore_signal(told.at[sides[i][1]], 1, device_id=sides[i][0], device_id_type=MESH)
-        for i in at:
-            pl.semaphore_wait(told.at[i], 1)
+        if n == 1:
+            pl.when(z == 0)(lambda: pl.semaphore_wait(bar, 1))
+        hear(n - 1)
+        for peer, i, far in sides:
+            if far > n:
+                pl.semaphore_signal(told.at[i], 1, device_id=peer, device_id_type=MESH)
+
+    given = []
+
+    def give(src, dst):
+        cp = pltpu.make_async_copy(src, dst, out_s.at[len(given)])
+        cp.start()
+        given.append(cp)
 
     def remote(src, dst, ss, rs, dev):
         return pltpu.make_async_remote_copy(
@@ -188,26 +216,31 @@
                 for p in (2 * u + 1, 2 * u):
                     half = term[:, (p % 2) * HF : (p % 2) * HF + HF].astype(BF16)
                     half = half.reshape(X, Z, -1, HF)
-                    if p == ZFIRST:
+                    if p in ZFIRST:
                         for i in range(X):
                             for j in range(Z):
-                                Gz[j, i] = half[i, j]
+                                Gz[p, j, i] = half[i, j]
                         for i in range(1, Z):
-                            go(z_first(i))
+                            go(z_first(p, i))
                     else:
                         Gs[p] = half
                         for i in range(1, X):
                             go(xstage(p, i))
 
         grads(0, xc, dhb, U)
-        if last:
-            wuu = (wu[...].astype(F32) * U[...]).astype(BF16)
-            gv = nt_dot(jnp.ones((8, FH), BF16), wuu)
-            for j in range(Y):
-                g1[j] = gv[:, j * 128 : (j + 1) * 128]
-            go(gacopy())
         grads(1, dc, act, V)
-        q = nn_dot(wg[...], dhb) - B[k, :, 0:FB, :].reshape(D, TC).astype(F32) * ct
+        DH[k] = dhb
+        CT[k] = ct
+
+    def gain_start():
+        wuu = (wu[...].astype(F32) * U[...]).astype(BF16)
+        gv = nt_dot(jnp.ones((8, FH), BF16), wuu)
+        for j in range(Y):
+            g1[j] = gv[:, j * 128 : (j + 1) * 128]
+        go(gacopy())
+
+    def terms(k):
+        q = nn_dot(wg[...], DH[k]) - B[k, :, 0:FB, :].reshape(D, TC).astype(F32) * CT[k]
         q = q.astype(BF16)
         for j in range(2 * Y):
             Q[k, j % 2, j // 2] = q[j * FB : (j + 1) * FB, :]
@@ -229,16 +262,14 @@
             Ss.at[p, (z + i) % Z], Zr.at[p, i - 1], z_s.at[p, i - 1], z_r.at[p, i - 1], zdev(i)
         )
 
-    def z_first(i):
-        p = ZFIRST
+    def z_first(p, i):
         return remote(
-            Gz.at[(z + i) % Z], Zf.at[i - 1], z_s.at[p, i - 1], z_r.at[p, i - 1], zdev(i)
+            Gz.at[p, (z + i) % Z], Zf.at[p, i - 1], z_s.at[p, i - 1], z_r.at[p, i - 1], zdev(i)
         )
 
-    def x_second(i):
-        p = ZFIRST
+    def x_second(p, i):
         return remote(
-            Sx.at[(x + i) % X], Xf.at[i - 1], x_s.at[p, i - 1], x_r.at[p, i - 1], xdev(i)
+            Sx.at[p, (x + i) % X], Xf.at[p, i - 1], x_s.at[p, i - 1], x_r.at[p, i - 1], xdev(i)
         )
 
     def rs(d, h, k):
@@ -284,7 +315,9 @@
     def rs_end(k):
         tot = both(y, k) + came(0, 1, k) + came(1, 1, k)
         tot = B[k, m, FB : 2 * FB, :].astype(F32) + tot
-        dtok_ref[:, pl.ds(k * TC, TC)] = (tot * live_s[k]).astype(BF16)
+        lanes = pl.ds(k * TC, TC)
+        dtok_ref[:, lanes] = (tot * live_s[k]).astype(BF16)
+        give(dtok_ref.at[:, lanes], dtok_out.at[:, lanes])
 
     def gain_a():
         gacopy().wait_recv()
@@ -326,16 +359,17 @@
             t = t + gz[i - 1]
         t = t * s
         dgain_ref[...] = jnp.where(c == 0, t[0:1, 0:FB], t[0:1, FB : 2 * FB])
+        give(dgain_ref, dgain_out)
 
     def first_end(p):
-        if p == ZFIRST:
-            t = Gz[z].astype(F32)
+        if p in ZFIRST:
+            t = Gz[p, z].astype(F32)
             for i in range(1, Z):
-                z_first(i).wait_recv()
-                t = t + Zf[i - 1].astype(F32)
-            Sx[...] = t.astype(BF16)
+                z_first(p, i).wait_recv()
+                t = t + Zf[p, i - 1].astype(F32)
+            Sx[p] = t.astype(BF16)
             for i in range(1, X):
-                go(x_second(i))
+                go(x_second(p, i))
         else:
             t = Gs[p, x].astype(F32)
             for i in range(1, X):
@@ -346,11 +380,11 @@
                 go(zstage(p, i))
 
     def second_end(p):
-        if p == ZFIRST:
-            t = Sx[x].astype(F32)
+        if p in ZFIRST:
+            t = Sx[p, x].astype(F32)
             for i in range(1, X):
-                x_second(i).wait_recv()
-                t = t + Xf[i - 1].astype(F32)
+                x_second(p, i).wait_recv()
+                t = t + Xf[p, i - 1].astype(F32)
         else:
             t = Ss[p, z].astype(F32)
             for i in range(1, Z):
@@ -360,18 +394,26 @@
         lanes = pl.ds((p % 2) * HF, HF)
         if p < 2:
             dup_ref[:, lanes] = t * gainb[r]
+            give(dup_ref.at[:, lanes], dup_out.at[:, lanes])
         else:
             ddn_ref[:, lanes] = t
+            give(ddn_ref.at[:, lanes], ddn_out.at[:, lanes])
+
+    def calm():
+        for _ in range(NCH * (4 * H2 - 1)):
+            pending.pop(0).wait_send()
 
     def drain():
-        for cp in pending[:drained]:
-            cp.wait_send()
+        while pending:
+            pending.pop().wait_send()
 
     steps = {
         "own": lambda h, k: own_send(k),
         "prep": lambda h, k: prep(),
         "arrive": arrive,
         "compute": lambda h, k: compute(k),
+        "terms": lambda h, k: terms(k),
+        "gain": lambda h, k: gain_start(),
         "rs": rs_step,
         "rs_end": lambda h, k: rs_end(k),
         "first": lambda h, k: first_end(k),
@@ -381,14 +423,15 @@
         "gain_z": lambda h, k: gain_z(),
         "gain_end": lambda h, k: gain_end(),
         "drain": lambda h, k: drain(),
+        "calm": lambda h, k: calm(),
         "tell": lambda h, k: tell(h),
+        "hear": lambda h, k: hear(h),
     }
     for what, h, k in order_of(H2):
-        if what == "compute":
-            drained = len(pending) if k == 0 else drained
         steps[what](h, k)
-    for cp in pending[drained:]:
-        cp.wait_send()
+    drain()
+    for cp in given:
+        cp.wait()
 
 
 def hand_out(*refs):
@@ -418,7 +461,13 @@
         RW = D // R
         H2 = Y // 2
         dma = pltpu.SemaphoreType.DMA
-        scratch = [
+        shapes = [
+            jax.ShapeDtypeStruct((FB, T), BF16),
+            jax.ShapeDtypeStruct((RW, FH), F32),
+            jax.ShapeDtypeStruct((RW, FH), F32),
+            jax.ShapeDtypeStruct((1, FB), F32),
+        ]
+        scratch = [pltpu.VMEM(t.shape, t.dtype) for t in shapes] + [
             pltpu.SMEM((4,), jnp.int32),
             pltpu.VMEM((1, D), F32),
             pltpu.VMEM((NCH, M, 2 * FB, TC), BF16),
@@ -437,10 +486,12 @@
             pltpu.VMEM((4, X, Z, RW, HF), BF16),
             pltpu.VMEM((4, Z, RW, HF), BF16),
             pltpu.VMEM((4, Z, RW, HF), BF16),
-            pltpu.VMEM((Z, X, RW, HF), BF16),
-            pltpu.VMEM((Z, X, RW, HF), BF16),
-            pltpu.VMEM((X, RW, HF), BF16),
-            pltpu.VMEM((X, RW, HF), BF16),
+            pltpu.VMEM((4, Z, X, RW, HF), BF16),
+            pltpu.VMEM((4, Z, X, RW, HF), BF16),
+            pltpu.VMEM((4, X, RW, HF), BF16),
+            pltpu.VMEM((4, X, RW, HF), BF16),
+            pltpu.VMEM((NCH, FH, TC), BF16),
+            pltpu.VMEM((NCH, 1, TC), F32),
             pltpu.VMEM((Y, 8, 128), F32),
             pltpu.VMEM((Y, 8, 128), F32),
             pltpu.VMEM((Y, 8, 128), F32),
@@ -451,6 +502,7 @@
             pltpu.VMEM((Z, 8, 128), F32),
             pltpu.VMEM((NCH, 1, TC), F32),
             dma((2 * NCH + 4,)),
+            dma((NCH + 5,)),
             dma((2, H2, NCH)),
             dma((2, H2, NCH)),
             dma((Y, NCH)),
@@ -474,18 +526,11 @@
             pltpu.SemaphoreType.REGULAR((6,)),
         ]
         hbm = pl.BlockSpec(memory_space=pltpu.HBM)
-        vm = pl.BlockSpec(memory_space=pltpu.VMEM)
-        shapes = [
-            jax.ShapeDtypeStruct((FB, T), BF16),
-            jax.ShapeDtypeStruct((RW, FH), F32),
-            jax.ShapeDtypeStruct((RW, FH), F32),
-            jax.ShapeDtypeStruct((1, FB), F32),
-        ]
         sums = pl.pallas_call(
             functools.partial(kernel, X, Z, Y, s),
             out_shape=shapes,
             in_specs=[hbm] * 6,
-            out_specs=[vm, vm, vm, vm],
+            out_specs=[hbm] * 4,
             scratch_shapes=scratch,
             compiler_params=pltpu.CompilerParams(
                 collective_id=0, has_side_effects=True, vmem_limit_bytes=56 << 20

time: 64 us -> 61.9 us (0.967)
  the two profiles are of different devices: /device:TPU:64 before, /device:TPU:1 now
where the time goes in v4:
time: 61.9 us; the launch traced here: 61.6 us
  Pallas kernels  61 us (99%)
  between operations  0.64 us (1%)
    pallas_call x1, Pallas kernels, on_device(): pl.pallas_call(functools.partial(kernel, X, Z, Y, s), out_shape=shapes, i...  59.3 us
    pallas_call x1, Pallas kernels, on_device(): pl.pallas_call(hand_out, out_shape=shapes, in_specs=[hbm] * 4, out_specs=...  1.64 us

profile of v4, /device:TPU:1, one launch (start us, length us, event | category | flops | bytes accessed | tf_op | source)
XLA Modules:
  0.0 61.6 jit_solution(69492254506621880)
XLA Ops:
  0.6 59.3 %shard_map.93 = (bf16[64,1024]{1,0:T(8,128)(2,1)}, f32[32,256]{1,0:T(8,128)}, f32[32,256]{1,0:T(8,128)}, f32[1,64]{1,0:T(1,128)}) custom-call(bf16[64,1024]{1,0:T(8,128)(2,1)} %bitcast.6, bf16[64,1024]{1,0:T(8,128)(2,1)} %bitcast.7, f32[1,1024]{1,0:T(1,128)} %bitcast.10, bf16[1024,256]{1,0:T(8,128)(2,1)} %wu_hbm.1, bf16[256,1024]{1,0:T(8,128)(2,1)} %wd_hbm.1, ...), custom_call_target="tpu_custom_call" | custom-call | flops 2684354560 | bytes 4194304 | tf_op jit(solution)/shard_map/pallas_call | solution.py:529
  59.9 1.6 %shard_map.94 = (bf16[64,1024]{1,0:T(8,128)(2,1)}, f32[32,256]{1,0:T(8,128)}, f32[32,256]{1,0:T(8,128)}, f32[1,64]{1,0:T(1,128)}) custom-call(bf16[64,1024]{1,0:T(8,128)(2,1)} %get-tuple-element.12.refs_0_, f32[32,256]{1,0:T(8,128)} %get-tuple-element.13.refs_1_, f32[32,256]{1,0:T(8,128)} %get-tuple-element.14.refs_2_, f32[1,64]{1,0:T(1,128)} %get-tuple-element.15.refs_3_), custom_call_target="tpu_custom_call" | custom-call | tf_op jit(solution)/shard_map/pallas_call | solution.py:542

commit v5 on v4

--- a/solution.py
+++ b/solution.py
@@ -38,7 +38,7 @@
         seq.append(("arrive", H2, k))
         if 1 <= k < last:
             seq.append(("compute", 0, k - 1))
-    seq.append(("hear", H2 - 1, 0))
+    seq += [("hear", H2 - 1, 0), ("upper", 0, 0)]
     far = [[("rs", H2, k), ("rs", H2 - 1, k)] for k in range(NCH)]
     near = [("rs", h, k) for h in range(H2 - 2, 0, -1) for k in range(NCH)]
     term = [("terms", 0, k) for k in range(NCH)]
@@ -46,9 +46,9 @@
     two = {p: ("second", 0, p) for p in range(4)}
     seq += [("compute", 0, last - 1), ("compute", 0, last), ("gain", 0, 0)]
     seq += [term[0], ("gain_a", 0, 0), term[1]] + far[0] + [term[2]] + far[1]
-    seq += [one[0], ("calm", 0, 0), ("gain_x", 0, 0), term[3]] + far[2] + far[3]
-    seq += [one[3], near[0], one[1], near[1], ("gain_z", 0, 0), near[2], one[2], near[3]]
-    seq += near[4:] + [("rs_end", 0, k) for k in range(NCH)]
+    seq += [one[0], term[3]] + far[2] + far[3] + [("gain_x", 0, 0), ("calm", 0, 0)]
+    seq += [one[3], near[0], near[1], one[2], near[2], near[3], ("gain_z", 0, 0)]
+    seq += near[4:6] + [one[1]] + near[6:] + [("rs_end", 0, k) for k in range(NCH)]
     seq += [two[0], two[3], ("gain_end", 0, 0), ("drain", 0, 0), two[1], two[2]]
     return seq
 
@@ -84,16 +84,23 @@
         return (x * Z + (z + k + Z) % Z, m)
 
     bar = pltpu.get_barrier_semaphore()
-    sides = [(ydev(1), 1, H2), (ydev(-1), 0, H2), (zdev(1), 3, Z // 2), (zdev(-1), 2, Z // 2)]
-    sides += [(xdev(1), 5, X // 2), (xdev(-1), 4, X // 2)]
+    sides = [(ydev(1), 1, H2), (ydev(-1), 0, H2), (xdev(1), 3, X // 2), (xdev(-1), 2, X // 2)]
 
     def greet(p):
         pl.semaphore_signal(bar, 1, device_id=p, device_id_type=MESH)
 
-    for p in [sib, ydev(1), ydev(-1), xdev(1), xdev(-1)]:
+    half = Z // 2
+    low = z < half
+    base = z - z % half
+
+    def zmate(k):
+        return (x * Z + base + (z + k) % half, m)
+
+    def zacross(k):
+        return (x * Z + half - base + k, m)
+
+    for p in [sib, ydev(1), ydev(-1), xdev(1), xdev(-1)] + [zmate(k) for k in range(1, half)]:
         greet(p)
-    pl.when(z < Z - 1)(lambda: greet(zdev(1)))
-    pl.when(z > 0)(lambda: greet(zdev(-1)))
 
     own = []
     for k in range(NCH):
@@ -115,21 +122,22 @@
         live_s[k] = jnp.where(at < load, 1.0, 0.0).astype(F32)
     for cp in own:
         cp.wait()
-    pl.when(z == 0)(lambda: pl.semaphore_wait(bar, 6))
-    pl.when(z > 0)(lambda: pl.semaphore_wait(bar, 7))
-    pl.when(z == 0)(lambda: greet(zdev(-1)))
-    pl.when(z == Z - 1)(lambda: greet(zdev(1)))
+    pl.when(low)(lambda: pl.semaphore_wait(bar, 4 + half))
+    pl.when(z >= half)(lambda: pl.semaphore_wait(bar, 4 + 2 * half))
+    for k in range(half):
+        greet(zacross(k))
 
     pending = []
 
     def hear(n):
-        for i in range(6):
+        for i in range(4):
             if sides[i][2] > n > 0:
                 pl.semaphore_wait(told.at[i], 1)
 
+    def upper_in():
+        pl.when(low)(lambda: pl.semaphore_wait(bar, half))
+
     def tell(n):
-        if n == 1:
-            pl.when(z == 0)(lambda: pl.semaphore_wait(bar, 1))
         hear(n - 1)
         for peer, i, far in sides:
             if far > n:
@@ -426,6 +434,7 @@
         "calm": lambda h, k: calm(),
         "tell": lambda h, k: tell(h),
         "hear": lambda h, k: hear(h),
+        "upper": lambda h, k: upper_in(),
     }
     for what, h, k in order_of(H2):
         steps[what](h, k)
@@ -523,7 +532,7 @@
             dma((X,)),
             dma((Z,)),
             dma((Z,)),
-            pltpu.SemaphoreType.REGULAR((6,)),
+            pltpu.SemaphoreType.REGULAR((4,)),
         ]
         hbm = pl.BlockSpec(memory_space=pltpu.HBM)
         sums = pl.pallas_call(

time: 61.9 us -> 62 us (level)
  no operation moved by 1% of the time
where the time goes in v5:
time: 62 us; the launch traced here: 61.9 us
  Pallas kernels  61.2 us (99%)
  between operations  0.64 us (1%)
    pallas_call x1, Pallas kernels, on_device(): pl.pallas_call(functools.partial(kernel, X, Z, Y, s), out_shape=shapes, i...  59.6 us
    pallas_call x1, Pallas kernels, on_device(): pl.pallas_call(hand_out, out_shape=shapes, in_specs=[hbm] * 4, out_specs=...  1.64 us

profile of v5, /device:TPU:1, one launch (start us, length us, event | category | flops | bytes accessed | tf_op | source)
XLA Modules:
  0.0 61.9 jit_solution(574832887999550730)
XLA Ops:
  0.6 59.6 %shard_map.93 = (bf16[64,1024]{1,0:T(8,128)(2,1)}, f32[32,256]{1,0:T(8,128)}, f32[32,256]{1,0:T(8,128)}, f32[1,64]{1,0:T(1,128)}) custom-call(bf16[64,1024]{1,0:T(8,128)(2,1)} %bitcast.6, bf16[64,1024]{1,0:T(8,128)(2,1)} %bitcast.7, f32[1,1024]{1,0:T(1,128)} %bitcast.10, bf16[1024,256]{1,0:T(8,128)(2,1)} %wu_hbm.1, bf16[256,1024]{1,0:T(8,128)(2,1)} %wd_hbm.1, ...), custom_call_target="tpu_custom_call" | custom-call | flops 2684354560 | bytes 4194304 | tf_op jit(solution)/shard_map/pallas_call | solution.py:538
  60.2 1.6 %shard_map.94 = (bf16[64,1024]{1,0:T(8,128)(2,1)}, f32[32,256]{1,0:T(8,128)}, f32[32,256]{1,0:T(8,128)}, f32[1,64]{1,0:T(1,128)}) custom-call(bf16[64,1024]{1,0:T(8,128)(2,1)} %get-tuple-element.12.refs_0_, f32[32,256]{1,0:T(8,128)} %get-tuple-element.13.refs_1_, f32[32,256]{1,0:T(8,128)} %get-tuple-element.14.refs_2_, f32[1,64]{1,0:T(1,128)} %get-tuple-element.15.refs_3_), custom_call_target="tpu_custom_call" | custom-call | tf_op jit(solution)/shard_map/pallas_call | solution.py:551

commit v6 on v5

--- a/solution.py
+++ b/solution.py
@@ -59,7 +59,7 @@
     dtok_out, dup_out, ddn_out, dgain_out,
     dtok_ref, dup_ref, ddn_ref, dgain_ref,
     counts_ref, gain_ref, B, wu, wd, wg, wgT, gainb, Q, Qs, RSs, RSr, U, V, Gs, Xr, Ss, Zr, Gz, Zf, Sx, Xf,
-    DH, CT, g1, g1r, g2, gy, g3, gx, g4, gz, live_s,
+    DH, CT, AC, g1, g1r, g2, gy, g3, gx, g4, gz, live_s,
     loc, out_s, ag_s, ag_r, sb_s, sb_r, qs_s, qs_r, rs_s, rs_r, x_s, x_r, z_s, z_r,
     ga_s, ga_r, gy_s, gy_r, gx_s, gx_r, gz_s, gz_r, told,
 ):
@@ -215,11 +215,20 @@
         ct = jnp.sum(dh * v, axis=0, keepdims=True) * inv * (1.0 / D)
         dhb = dh.astype(BF16)
 
-        def grads(u, lhs, rhs, acc):
-            term = nt_dot(lhs, rhs)
-            if k > 0:
+        DH[k] = dhb
+        CT[k] = ct
+        AC[k] = act
+        if k % 2 == 0:
+            return
+
+        def grads(u, rhs, acc):
+            rows = pl.ds(u * FB, FB)
+            term = nt_dot(B[k - 1, :, rows, :].reshape(D, TC), rhs[k - 1])
+            term = term + nt_dot(B[k, :, rows, :].reshape(D, TC), rhs[k])
+            if k > 1:
                 term = acc[...] + term
-            acc[...] = term
+            if not last or u == 0:
+                acc[...] = term
             if last:
                 for p in (2 * u + 1, 2 * u):
                     half = term[:, (p % 2) * HF : (p % 2) * HF + HF].astype(BF16)
@@ -235,10 +244,8 @@
                         for i in range(1, X):
                             go(xstage(p, i))
 
-        grads(0, xc, dhb, U)
-        grads(1, dc, act, V)
-        DH[k] = dhb
-        CT[k] = ct
+        grads(0, DH, U)
+        grads(1, AC, V)
 
     def gain_start():
         wuu = (wu[...].astype(F32) * U[...]).astype(BF16)
@@ -501,6 +508,7 @@
             pltpu.VMEM((4, X, RW, HF), BF16),
             pltpu.VMEM((NCH, FH, TC), BF16),
             pltpu.VMEM((NCH, 1, TC), F32),
+            pltpu.VMEM((NCH, FH, TC), BF16),
             pltpu.VMEM((Y, 8, 128), F32),
             pltpu.VMEM((Y, 8, 128), F32),
             pltpu.VMEM((Y, 8, 128), F32),

time: 62 us -> 62.4 us (level)
  no operation moved by 1% of the time
where the time goes in v6:
time: 62.4 us; the launch traced here: 62.3 us
  Pallas kernels  61.6 us (99%)
  between operations  0.64 us (1%)
    pallas_call x1, Pallas kernels, on_device(): pl.pallas_call(functools.partial(kernel, X, Z, Y, s), out_shape=shapes, i...  60 us
    pallas_call x1, Pallas kernels, on_device(): pl.pallas_call(hand_out, out_shape=shapes, in_specs=[hbm] * 4, out_specs=...  1.64 us

profile of v6, /device:TPU:1, one launch (start us, length us, event | category | flops | bytes accessed | tf_op | source)
XLA Modules:
  0.0 62.3 jit_solution(52036527074903294)
XLA Ops:
  0.6 60.0 %shard_map.93 = (bf16[64,1024]{1,0:T(8,128)(2,1)}, f32[32,256]{1,0:T(8,128)}, f32[32,256]{1,0:T(8,128)}, f32[1,64]{1,0:T(1,128)}) custom-call(bf16[64,1024]{1,0:T(8,128)(2,1)} %bitcast.6, bf16[64,1024]{1,0:T(8,128)(2,1)} %bitcast.7, f32[1,1024]{1,0:T(1,128)} %bitcast.10, bf16[1024,256]{1,0:T(8,128)(2,1)} %wu_hbm.1, bf16[256,1024]{1,0:T(8,128)(2,1)} %wd_hbm.1, ...), custom_call_target="tpu_custom_call" | custom-call | flops 2684354560 | bytes 4194304 | tf_op jit(solution)/shard_map/pallas_call | solution.py:546
  60.6 1.6 %shard_map.94 = (bf16[64,1024]{1,0:T(8,128)(2,1)}, f32[32,256]{1,0:T(8,128)}, f32[32,256]{1,0:T(8,128)}, f32[1,64]{1,0:T(1,128)}) custom-call(bf16[64,1024]{1,0:T(8,128)(2,1)} %get-tuple-element.12.refs_0_, f32[32,256]{1,0:T(8,128)} %get-tuple-element.13.refs_1_, f32[32,256]{1,0:T(8,128)} %get-tuple-element.14.refs_2_, f32[1,64]{1,0:T(1,128)} %get-tuple-element.15.refs_3_), custom_call_target="tpu_custom_call" | custom-call | tf_op jit(solution)/shard_map/pallas_call | solution.py:559
